TPU v7x, 512 devices: a whole 4x4x16 slice. The times are simulated.
512 devices in a mesh: seq: 64 (over z, y), head: 8 (over x, core).
Axes of the slice: x: 4, y: 4, z: 16, core: 2. Of those that a mesh axis runs over, the one named last changes fastest.
Arguments:
- store_hidden: bfloat16 [16384, 8192], P('seq', 'head'), may hold values from -320 to 320
- owner_map: int32 [16384, 1], P('seq'), may hold values from 0 to 63, as said below
- new_hidden: bfloat16 [8192, 8192], P('seq', 'head'), may hold values from -320 to 320
- new_lengths: int32 [64], P('seq'), may hold values from 1 to 128, as said below
- queries: bfloat16 [8192, 8192], P('seq', 'head'), may hold values from -240 to 240
- key_weight: bfloat16 [8192, 1024], P('head', 'seq'), may hold values from -0.013671875 to 0.013671875
- value_weight: bfloat16 [8192, 1024], P('head', 'seq'), may hold values from -0.013671875 to 0.013671875
Outputs:
- attended: bfloat16 [8192, 8192], P('seq', 'head')
- key_cache: bfloat16 [64, 640, 1024], P('seq', None, 'head')
- value_cache: bfloat16 [64, 640, 1024], P('seq', None, 'head')
Inputs may be any that keep to these rules, and one draw needn't show every extreme that they name: `owner_map`: within the 256 rows of one store shard no session owns more than 8 rows; in every draw one session owns exactly 8 rows of every shard, so its history is 512 rows; every session owns at least one row. `new_lengths`: some session's new turn has exactly 128 tokens.
All inputs are finite; a program needn't handle non-finite values.
Results may differ from a plain program's by a relative error of at most 0.033.
Values may be sent and summed in bfloat16 or wider, within the bound.
A program may use at most 64 MiB of HBM per device.

v0:
```python
import math

import jax
import jax.numpy as jnp
from jax import lax
from jax.sharding import PartitionSpec as P

D = 8192
QH = 64
KVH = 8
HD = 128


rope_base = 500000.0


def frequencies():
    half_index = jnp.arange(HD // 2, dtype=jnp.float32)
    inverse = 1.0 / jnp.power(rope_base, 2.0 * half_index / HD)
    wavelength = 2.0 * jnp.pi / inverse
    smooth = (8192.0 / wavelength - 1.0) / 3.0
    mixed = (1.0 - smooth) * inverse / 8.0 + smooth * inverse
    return jnp.where(
        wavelength < 2048.0, inverse, jnp.where(wavelength > 8192.0, inverse / 8.0, mixed)
    )


def rotate(values, angles):
    cosine = jnp.cos(angles)
    sine = jnp.sin(angles)
    first = values[..., : HD // 2]
    second = values[..., HD // 2 :]
    return jnp.concatenate(
        [first * cosine - second * sine, second * cosine + first * sine], axis=-1
    )


def place_rows(received, arrived_meta, history):
    sessions = received.shape[0]
    capacity = received.shape[1]
    slot_index = jnp.arange(capacity, dtype=jnp.int32)
    target = jnp.where(
        slot_index[None, :] < arrived_meta[:, 0:1],
        arrived_meta[:, 1:2] + slot_index[None, :],
        history,
    )
    flat_rows = received.reshape((sessions * capacity,) + received.shape[2:])
    empty_rows = jnp.zeros((history,) + received.shape[2:], received.dtype)
    return empty_rows.at[target.reshape(-1)].set(flat_rows, mode="drop")


def local(store_hidden, owner_map, new_hidden, new_lengths, queries, key_weight, value_weight):
    sessions = lax.axis_size("seq")
    local_heads = KVH // lax.axis_size("head")
    stored_rows = store_hidden.shape[0]
    capacity = 2 * stored_rows // sessions
    history = 2 * stored_rows
    turn_rows = new_hidden.shape[0]
    frequency = frequencies()
    key_full, value_full = (
        lax.all_gather(key_weight, "seq", axis=1, tiled=True),
        lax.all_gather(value_weight, "seq", axis=1, tiled=True),
    )
    key_heads = key_full.reshape(key_full.shape[0], KVH, HD)
    value_heads = value_full.reshape(value_full.shape[0], KVH, HD)
    owners = owner_map[:, 0]
    owner_hits = (owners[:, None] == jnp.arange(sessions, dtype=jnp.int32)[None, :]).astype(
        jnp.int32
    )
    row_ranks = jnp.sum((jnp.cumsum(owner_hits, axis=0) - owner_hits) * owner_hits, axis=1)
    owner_counts = jnp.sum(owner_hits, axis=0)
    outgoing = (
        jnp.zeros((sessions, capacity, store_hidden.shape[1]), jnp.bfloat16)
        .at[owners, row_ranks]
        .set(store_hidden)
    )
    received, arrived_counts = (
        lax.all_to_all(outgoing, "seq", split_axis=0, concat_axis=0, tiled=True),
        lax.all_to_all(owner_counts[:, None], "seq", split_axis=0, concat_axis=0, tiled=True),
    )
    source_starts = jnp.cumsum(arrived_counts[:, 0]) - arrived_counts[:, 0]
    length = jnp.sum(arrived_counts[:, 0])
    arrived_meta = jnp.concatenate([arrived_counts, source_starts[:, None]], axis=1)
    gathered = place_rows(received, arrived_meta, history)
    hidden_rows = jnp.concatenate([gathered, new_hidden], axis=0)
    squares = jnp.sum(jnp.square(hidden_rows.astype(jnp.float32)), axis=1)
    totals = lax.psum(squares, "head")
    scales = lax.rsqrt(totals / D + 1e-05)
    key_term = jnp.einsum("rf,fkh->krh", hidden_rows, key_heads, preferred_element_type=jnp.float32)
    value_term = jnp.einsum(
        "rf,fkh->krh", hidden_rows, value_heads, preferred_element_type=jnp.float32
    )
    summed = lax.psum_scatter(
        jnp.concatenate([key_term, value_term], axis=2).astype(jnp.bfloat16),
        "head",
        scatter_dimension=0,
        tiled=True,
    ).astype(jnp.float32)
    projected = summed * scales[None, :, None]
    history_part = projected[:, :history]
    positions = jnp.arange(history, dtype=jnp.int32)
    history_angles = positions.astype(jnp.float32)[None, :, None] * frequency[None, None, :]
    history_keys = rotate(history_part[..., :HD], history_angles).astype(jnp.bfloat16)
    history_values = history_part[..., HD:].astype(jnp.bfloat16)
    fresh_rows = projected[:, history:]
    turn_index = jnp.arange(turn_rows, dtype=jnp.int32)
    live_rows = turn_index < new_lengths[0]
    fresh_angles = (length + turn_index).astype(jnp.float32)[:, None] * frequency[None, :]
    fresh_keys = jnp.where(
        live_rows[None, :, None], rotate(fresh_rows[..., :HD], fresh_angles[None]), 0.0
    ).astype(jnp.bfloat16)
    fresh_values = jnp.where(live_rows[None, :, None], fresh_rows[..., HD:], 0.0).astype(
        jnp.bfloat16
    )
    keys = jnp.concatenate([history_keys, fresh_keys], axis=1)
    values = jnp.concatenate([history_values, fresh_values], axis=1)
    cache_rows = keys.shape[1]
    group = QH // KVH
    query_heads = queries.reshape(turn_rows, local_heads, group, HD).astype(jnp.float32)
    rotated_queries = rotate(query_heads, fresh_angles[:, None, None, :]).astype(jnp.bfloat16)
    scores = jnp.einsum(
        "jkgh,kch->kgjc", rotated_queries, keys, preferred_element_type=jnp.float32
    ) / math.sqrt(HD)
    column = jnp.arange(cache_rows, dtype=jnp.int32)
    allowed = (column[None, :] < length) | (column[None, :] >= history) & (
        column[None, :] - history <= turn_index[:, None]
    )
    scores = jnp.where(allowed[None, None], scores, -jnp.inf)
    highest = jnp.max(scores, axis=-1, keepdims=True)
    exponent = jnp.exp(scores - highest)
    attention_weights = (exponent / jnp.sum(exponent, axis=-1, keepdims=True)).astype(jnp.bfloat16)
    result = jnp.einsum(
        "kgjc,kch->jkgh", attention_weights, values, preferred_element_type=jnp.float32
    )
    result = jnp.where(live_rows[:, None, None, None], result, 0.0).astype(jnp.bfloat16)
    attended = result.reshape(turn_rows, local_heads * group * HD)
    key_cache = jnp.transpose(keys, (1, 0, 2)).reshape(1, cache_rows, local_heads * HD)
    value_cache = jnp.transpose(values, (1, 0, 2)).reshape(1, cache_rows, local_heads * HD)
    return (attended, key_cache, value_cache)


def solution(mesh):
    placed = (
        P("seq", "head"),
        P("seq", None),
        P("seq", "head"),
        P("seq"),
        P("seq", "head"),
        P("head", "seq"),
        P("head", "seq"),
    )
    return jax.shard_map(
        local,
        mesh=mesh,
        in_specs=placed,
        out_specs=(P("seq", "head"), P("seq", None, "head"), P("seq", None, "head")),
        check_vma=False,
    )
```

profile of v0, /device:TPU:1, one launch (start us, length us, event | category | flops | bytes accessed | tf_op | source)
XLA Modules:
  0.0 362.6 jit_solution(17163967799993898027)
XLA Ops:
  7.2 0.7 all-gather.3.cloned.1.call-update
  7.9 0.7 fusion.39
  8.6 0.6 reduce-window.19
  9.4 0.9 fusion.36
  10.3 0.7 copy.37
  11.0 19.3 %all-to-all-start = ((s32[64,1,1]{2,1,0:T(1,128)}), s32[64,1,1]{2,1,0:T(1,128)S(1)}, u32[]{:S(2)}, u32[]{:S(2)}) async-start(s32[64,1,1]{2,1,0:T(1,128)} %copy.37), calls=%async_computation | async-start | bytes 65536 | tf_op jit(solution)/shard_map/all_to_all | solution.py:79
  30.3 0.7 or_select_fusion
  31.0 1.1 broadcast_in_dim.81
  32.1 36.7 %scatter_fusion = bf16[64,8,1024]{2,1,0:T(8,128)(2,1)} fusion(bf16[64,8,1024]{2,1,0:T(8,128)(2,1)} %broadcast_in_dim.81, s32[256]{0:T(256)S(1)} %bitcast.93, bf16[256,1024]{1,0:T(8,128)(2,1)} %param.7), kind=kCustom, calls=%fused_computation | custom fusion | bytes 1574912 | tf_op jit(solution)/shard_map/scatter | solution.py:75
  68.8 14.5 %all-to-all-start.1 = ((bf16[64,8,1024]{2,1,0:T(8,128)(2,1)}), bf16[64,8,1024]{2,1,0:T(8,128)(2,1)S(1)}, u32[]{:S(2)}, u32[]{:S(2)}) async-start(bf16[64,8,1024]{2,1,0:T(8,128)(2,1)} %scatter_fusion), calls=%async_computation.1 | async-start | bytes 2097152 | tf_op jit(solution)/shard_map/all_to_all | solution.py:78
  83.4 0.7 all-gather.5.cloned.1.call-update
  84.4 1.8 fusion.50
  86.4 52.8 %all-to-all-done.1 = bf16[64,8,1024]{2,1,0:T(8,128)(2,1)S(1)} async-done(((bf16[64,8,1024]{2,1,0:T(8,128)(2,1)}), bf16[64,8,1024]{2,1,0:T(8,128)(2,1)S(1)}, u32[]{:S(2)}, u32[]{:S(2)}) %all-to-all-start.1) | async-done | bytes 1048608 | tf_op jit(solution)/shard_map/all_to_all | solution.py:78
  139.1 2.8 scatter_custom_fusion.1
  142.1 18.3 %all-gather.3.cloned.1.call-done = bf16[1024,1024]{0,1:T(8,128)(2,1)} async-done(((bf16[1024,16]{0,1:T(8,128)(2,1)}), bf16[1024,1024]{0,1:T(8,128)(2,1)}) %all-gather.3.cloned.1.call-update) | async-done | bytes 2097168 | tf_op jit(solution)/shard_map/all_gather | solution.py:61
  160.4 4.9 %fusion.52 = f32[640,1024]{0,1} fusion(bf16[640,1024]{1,0:T(8,128)(2,1)S(1)} %constant_dynamic-update-slice_fusion, bf16[1024,1024]{0,1:T(8,128)(2,1)} %all-gather.3.cloned.1.call-done), kind=kOutput, calls=%fused_computation.96 | convolution fusion | flops 1342177280 | bytes 6029312
  165.3 133.2 %all-gather.5.cloned.1.call-done = bf16[1024,1024]{0,1:T(8,128)(2,1)} async-done(((bf16[1024,16]{0,1:T(8,128)(2,1)}), bf16[1024,1024]{0,1:T(8,128)(2,1)}) %all-gather.5.cloned.1.call-update) | async-done | bytes 2097168 | tf_op jit(solution)/shard_map/all_gather | solution.py:62
  298.5 3.6 fusion.53
  302.4 1.8 pad_maximum_fusion
  305.9 0.7 add_convert_fusion.1
  306.5 0.7 iota_compare_fusion.4
  308.0 0.3 multiply_reduce_fusion
  308.3 21.5 %psum.7 = f32[640]{0:T(1024)S(1)} all-reduce(f32[640]{0:T(1024)S(1)} %multiply_reduce_fusion), channel_id=1, replica_groups=mesh['seq'=64,'head'=8] {'head'}, use_global_device_ids=true, to_apply=%region_9.10 | all-reduce | flops 640 | bytes 5120 | tf_op jit(solution)/shard_map/psum | solution.py:87
  329.8 19.9 %reduce-scatter.2.cloned.1.call-done = bf16[1,640,256]{1,2,0:T(8,128)(2,1)} async-done(((bf16[8,640,256]{1,2,0:T(8,128)(2,1)}), bf16[1,640,256]{1,2,0:T(8,128)(2,1)}) %reduce-scatter.2.cloned.1.call-update) | async-done | bytes 327696 | tf_op jit(solution)/shard_map/reduce_scatter | solution.py:93
  349.7 1.0 convert_multiply_fusion
  351.0 0.8 copy.47
  351.8 0.6 fusion.32
  352.4 0.8 copy.46
  353.2 0.6 fusion.1
  353.8 0.5 fusion
  354.4 0.9 fusion.11
  355.3 0.9 copy.45
  (40 shorter events, 3.1 us)
Async XLA Ops:
  7.2 153.2 %all-gather.3.cloned.1.call-start = ((), (), s32[]{:S(2)}) async-start(), calls=%async_computation.3 | async-start | bytes 2129920 | tf_op jit(solution)/shard_map/all_gather | solution.py:61
  11.0 57.8 %all-to-all-start = ((s32[64,1,1]{2,1,0:T(1,128)}), s32[64,1,1]{2,1,0:T(1,128)S(1)}, u32[]{:S(2)}, u32[]{:S(2)}) async-start(s32[64,1,1]{2,1,0:T(1,128)} %copy.37), calls=%async_computation | async-start | bytes 65536 | tf_op jit(solution)/shard_map/all_to_all | solution.py:79
  68.8 70.3 %all-to-all-start.1 = ((bf16[64,8,1024]{2,1,0:T(8,128)(2,1)}), bf16[64,8,1024]{2,1,0:T(8,128)(2,1)S(1)}, u32[]{:S(2)}, u32[]{:S(2)}) async-start(bf16[64,8,1024]{2,1,0:T(8,128)(2,1)} %scatter_fusion), calls=%async_computation.1 | async-start | bytes 2097152 | tf_op jit(solution)/shard_map/all_to_all | solution.py:78
  83.4 58.7 %copy-start.1 = (bf16[128,1024]{1,0:T(8,128)(2,1)S(1)}, bf16[128,1024]{1,0:T(8,128)(2,1)}, u32[]{:S(2)}) copy-start(bf16[128,1024]{1,0:T(8,128)(2,1)} %param.9) | copy-start | bytes 786436
  83.4 215.1 %all-gather.5.cloned.1.call-start = ((), (), s32[]{:S(2)}) async-start(), calls=%async_computation.4 | async-start | bytes 2129920 | tf_op jit(solution)/shard_map/all_gather | solution.py:62
  84.1 265.6 %reduce-scatter.2.cloned.1.call-start = ((), (), s32[]{:S(2)}) async-start(), calls=%async_computation.5 | async-start | bytes 2949120 | tf_op jit(solution)/shard_map/reduce_scatter | solution.py:93
  298.5 3.6 copy-start
  304.2 1.0 copy-start.2
Sparse Core Ops, SparseCore 0:
  10.9 149.4 all-gather.2
  163.3 135.1 all-gather.4
  304.3 45.3 reduce-scatter.1
where the time goes:
time: 365 us; the launch traced here: 363 us
  waiting for transfers between devices  226 us (62%)
  local copies, waits for them, and re-layouts  45.1 us (12%)
  starting transfers between devices  33.9 us (9%)
  blocking collectives  21.5 us (6%)
  between operations  14.7 us (4%)
  other arithmetic  11.9 us (3%)
  matrix products  9.96 us (3%)
    all_gather x1, waiting for transfers between devices, local(): lax.all_gather(value_weight, 'seq', axis=1, tiled=True)  133 us
    all_to_all x1, waiting for transfers between devices, local(): lax.all_to_all(outgoing, 'seq', split_axis=0, concat_axis=0, tiled=True)  52.8 us
    scatter x1, local copies, waits for them, and re-layouts, local(): outgoing = jnp.zeros((sessions, capacity, store_hidden.shape[1]), jnp.bfl...  36.7 us
    psum x1, blocking collectives, local(): totals = lax.psum(squares, 'head')  21.5 us
    reduce_scatter x1, waiting for transfers between devices, local(): lax.psum_scatter(jnp.concatenate([key_term, value_term], axis=2).astype(j...  19.9 us
    all_to_all x1, starting transfers between devices, local(): lax.all_to_all(owner_counts[:, None], 'seq', split_axis=0, concat_axis=0,...  19.3 us
    all_gather x1, waiting for transfers between devices, local(): lax.all_gather(key_weight, 'seq', axis=1, tiled=True)  18.3 us
    all_to_all x1, starting transfers between devices, local(): lax.all_to_all(outgoing, 'seq', split_axis=0, concat_axis=0, tiled=True)  14.5 us
  transfers between devices with their start and end apart: 5, of which 4 were waited for; matrix products, arithmetic and copies ran while one was open for 15% of the time, Pallas kernels for 0%

commit v1 on v0

v1 whole, which is shorter than its diff:
```python
import functools
import math

import jax
import jax.numpy as jnp
import numpy as np
from jax import lax
from jax.experimental import pallas as pl
from jax.experimental.pallas import tpu as pltpu
from jax.sharding import PartitionSpec as P

D = 8192
QH = 64
KVH = 8
HD = 128
NZ = 16
NY = 4
NX = 4
STORED = 256
TURN = 128
ROWS = STORED + TURN
CAP = 8
SESS = NZ * NY
HIST = SESS * CAP
CACHE = HIST + TURN
FEAT = D // (2 * NX)
CHIP_FEAT = 2 * FEAT
SPLIT = 1280
EMPTY = float(2.0**100)
EMPTY_TEST = float(2.0**50)
MESH = pl.DeviceIdType.MESH
rope_base = 500000.0


def rotation_tables():
    half_index = np.arange(HD // 2, dtype=np.float64)
    inverse = 1.0 / np.power(rope_base, 2.0 * half_index / HD)
    wavelength = 2.0 * np.pi / inverse
    smooth = (8192.0 / wavelength - 1.0) / 3.0
    mixed = (1.0 - smooth) * inverse / 8.0 + smooth * inverse
    frequency = np.where(
        wavelength < 2048.0, inverse, np.where(wavelength > 8192.0, inverse / 8.0, mixed)
    )
    angles = np.arange(CACHE, dtype=np.float64)[:, None] * frequency[None, :]
    cosine, sine = np.cos(angles), np.sin(angles)
    return (
        np.concatenate([cosine, cosine], axis=1).astype(np.float32),
        np.concatenate([-sine, sine], axis=1).astype(np.float32),
    )


def nt_dot(a, b):
    return lax.dot_general(a, b, (((1,), (1,)), ((), ())), preferred_element_type=jnp.float32)


def project_kernel(
    store_ref, owner_ref, new_ref, kw_ref, vw_ref,
    routed_ref, fresh_ref,
    xs, wl, gathered, partial, received, squares, onehot, outgoing, by_y, by_z,
    core_s, core_r, z_s, z_r, y_s, y_r, sum_s, sum_r, sq_s, sq_r, ry_s, ry_r, rz_s, rz_r,
):
    seq = lax.axis_index("seq")
    head = lax.axis_index("head")
    z, y = lax.div(seq, NY), lax.rem(seq, NY)
    x, c = lax.div(head, 2), lax.rem(head, 2)
    other = head + 1 - 2 * c

    def zp(delta):
        return lax.rem(z + delta + NZ, NZ)

    def yp(delta):
        return lax.rem(y + delta + NY, NY)

    def remote(src, dst, send_sem, recv_sem, to_seq, to_head):
        return pltpu.make_async_remote_copy(
            src_ref=src, dst_ref=dst, send_sem=send_sem, recv_sem=recv_sem,
            device_id=(to_seq, to_head), device_id_type=MESH,
        )

    sends = []

    def start(copy):
        copy.start()
        sends.append(copy)

    barrier = pltpu.get_barrier_semaphore()
    peers = [(seq, lax.rem(head + i, 2 * NX)) for i in range(1, 2 * NX)]
    peers += [(z * NY + yp(i), head) for i in range(1, NY)]
    peers += [(zp(i) * NY + y, head) for i in range(1, NZ)]
    for peer in peers:
        pl.semaphore_signal(barrier, inc=1, device_id=peer, device_id_type=MESH)

    own = pl.ds(pl.multiple_of(c * FEAT, FEAT), FEAT)
    theirs = pl.ds(pl.multiple_of((1 - c) * FEAT, FEAT), FEAT)
    wl[0] = kw_ref[...]
    wl[1] = vw_ref[...]
    gathered[z, y, :, own] = wl[c]
    xs[:STORED, own] = store_ref[...]
    xs[STORED:, own] = new_ref[...]
    pl.semaphore_wait(barrier, len(peers))

    start(remote(wl.at[1 - c], gathered.at[z, y, :, own], core_s.at[0], core_r.at[0], seq, other))
    start(remote(xs.at[:, own], xs.at[:, own], core_s.at[1], core_r.at[1], seq, other))
    remote(
        wl.at[1 - c], gathered.at[z, y, :, theirs], core_s.at[0], core_r.at[0], seq, other
    ).wait_recv()

    def z_region(flow, chunk):
        if flow == 0:
            return gathered.at[chunk, y, :, :SPLIT]
        return gathered.at[chunk, :, :, SPLIT:]

    def z_target(d):
        return zp(1 if d == 0 else -1) * NY + y

    def z_chunk(d, t):
        return zp(-t if d == 0 else t)

    def z_send(flow, d, t):
        region = z_region(flow, z_chunk(d, t - 1))
        start(remote(region, region, z_s.at[flow, d, t], z_r.at[flow, d, t], z_target(d), head))

    def z_wait(flow, d, t):
        region = z_region(flow, z_chunk(d, t))
        remote(region, region, z_s.at[flow, d, t], z_r.at[flow, d, t], z_target(d), head).wait_recv()

    def z_has(flow, d, t):
        return t < NZ // 2 or (t == NZ // 2 and flow == d)

    def y_target(d):
        return z * NY + yp(1 if d == 0 else -1)

    def y_copy(index, chunk, lo, hi, stage, d, delta):
        region = gathered.at[chunk, yp(delta), :, lo:hi]
        return remote(
            region, region, y_s.at[index, stage, d], y_r.at[index, stage, d], y_target(d), head
        )

    def y_one(index, chunk, lo, hi):
        for d in (0, 1):
            start(y_copy(index, chunk, lo, hi, 0, d, 0))

    def y_two(index, chunk, lo, hi):
        mid = (lo + hi) // 2
        y_copy(index, chunk, lo, hi, 0, 0, -1).wait_recv()
        start(y_copy(index, chunk, lo, mid, 1, 0, -1))
        y_copy(index, chunk, lo, hi, 0, 1, 1).wait_recv()
        start(y_copy(index, chunk, mid, hi, 1, 1, 1))

    def y_end(index, chunk, lo, hi):
        mid = (lo + hi) // 2
        y_copy(index, chunk, lo, mid, 1, 0, 2).wait_recv()
        y_copy(index, chunk, mid, hi, 1, 1, 2).wait_recv()

    def chunks_of(t):
        if t == 0:
            return [(0, z)]
        return [(2 * t + d, z_chunk(d, t)) for d in (0, 1) if z_has(0, d, t)]

    for d in (0, 1):
        z_send(0, d, 1)
    y_one(1, z, SPLIT, CHIP_FEAT)
    y_one(0, z, 0, SPLIT)

    ones = jnp.ones((8, 256), jnp.bfloat16)
    total = jnp.zeros((8, ROWS), jnp.float32)
    for piece in range(FEAT // 256):
        at = pl.ds(piece * 256, 256)
        block = jnp.concatenate([store_ref[:, at], new_ref[:, at]], axis=0).astype(jnp.float32)
        square = block * block
        high = square.astype(jnp.bfloat16)
        low = (square - high.astype(jnp.float32)).astype(jnp.bfloat16)
        total += nt_dot(ones, high) + nt_dot(ones, low)
    squares[head] = total
    for i in range(1, 2 * NX):
        to = lax.rem(head + i, 2 * NX)
        start(remote(squares.at[head], squares.at[head], sq_s.at[to], sq_r.at[head], seq, to))

    y_two(1, z, SPLIT, CHIP_FEAT)

    owner_row = owner_ref[...]
    owner_lanes = jnp.broadcast_to(owner_row.astype(jnp.float32), (STORED, STORED))
    earlier = lax.broadcasted_iota(jnp.int32, (STORED, STORED), 0) < lax.broadcasted_iota(
        jnp.int32, (STORED, STORED), 1
    )
    same = jnp.where(earlier & (owner_lanes.T == owner_lanes), 1.0, 0.0)
    rank = jnp.sum(same, axis=0, keepdims=True).astype(jnp.int32)
    owner_z = lax.shift_right_logical(owner_row, 2)
    owner_y = lax.bitwise_and(owner_row, 3)
    slot = (owner_y * NZ + owner_z) * CAP + rank
    onehot[...] = jnp.where(
        lax.broadcasted_iota(jnp.int32, (HIST, STORED), 0) == slot, 1.0, 0.0
    ).astype(jnp.bfloat16)

    remote(xs.at[:, theirs], xs.at[:, theirs], core_s.at[1], core_r.at[1], seq, other).wait_recv()

    def send_sum(chunk):
        to = lax.div(chunk, 2)
        half = lax.rem(chunk, 2)
        result = nt_dot(gathered[chunk].reshape(4 * 16, CHIP_FEAT), xs[...]).astype(jnp.bfloat16)
        partial[chunk] = result

        @pl.when(to == head)
        def _():
            received[x, c, half] = result

        @pl.when(to != head)
        def _():
            remote(
                partial.at[chunk], received.at[x, c, half],
                sum_s.at[chunk], sum_r.at[x, c, half], seq, to,
            ).start()

    last = NZ // 2
    for s in range(1, last + 3):
        if s <= last:
            for d in (0, 1):
                if z_has(0, d, s):
                    z_wait(0, d, s)
                    if z_has(0, d, s + 1):
                        z_send(0, d, s + 1)
                    y_one(2 * s + d, z_chunk(d, s), 0, SPLIT)
        if s == 1:
            y_end(1, z, SPLIT, CHIP_FEAT)
            for d in (0, 1):
                z_send(1, d, 1)
        elif s - 1 <= last:
            for d in (0, 1):
                if z_has(1, d, s - 1):
                    z_wait(1, d, s - 1)
                    if z_has(1, d, s):
                        z_send(1, d, s)
        if s - 1 <= last:
            for index, chunk in chunks_of(s - 1):
                y_two(index, chunk, 0, SPLIT)
        if s >= 2:
            for index, chunk in chunks_of(s - 2):
                y_end(index, chunk, 0, SPLIT)
                send_sum(chunk)

    for i in range(1, 2 * NX):
        frm = lax.rem(head + i, 2 * NX)
        remote(squares.at[frm], squares.at[frm], sq_s.at[frm], sq_r.at[frm], seq, frm).wait_recv()
    sums = jnp.sum(jnp.sum(squares[...], axis=0), axis=0, keepdims=True) * 0.125
    scale = lax.rsqrt(sums / D + 1e-05)
    for i in range(1, 2 * NX):
        frm = lax.rem(head + i, 2 * NX)
        fx, fc = lax.div(frm, 2), lax.rem(frm, 2)
        for half in (0, 1):
            remote(
                received.at[fx, fc, half], received.at[fx, fc, half],
                sum_s.at[0], sum_r.at[fx, fc, half], seq, frm,
            ).wait_recv()
    kinds = []
    for kind in (0, 1):
        summed = jnp.zeros((HD, ROWS), jnp.float32)
        for fx in range(NX):
            summed += received[fx, kind].reshape(HD, ROWS).astype(jnp.float32)
        scaled = summed * scale
        fresh_ref[kind] = scaled[:, STORED:]
        kinds.append(nt_dot(onehot[...], scaled[:, :STORED].astype(jnp.bfloat16)))
    filled = jnp.sum(onehot[...].astype(jnp.float32), axis=1, keepdims=True)
    keys = kinds[0] + (1.0 - filled) * EMPTY
    slots = jnp.concatenate(
        [keys.reshape(SESS, CAP, HD), kinds[1].reshape(SESS, CAP, HD)], axis=1
    )
    outgoing[...] = slots.astype(jnp.bfloat16).reshape(NY, NZ, 2 * CAP, HD)

    for i in (2, 1, 3):
        to = yp(i)
        start(remote(outgoing.at[to], by_y.at[y], ry_s.at[to], ry_r.at[y], z * NY + to, head))
    by_y[y] = outgoing[y]
    for i in (1, 3, 2):
        frm = yp(i)
        remote(outgoing.at[frm], by_y.at[frm], ry_s.at[frm], ry_r.at[frm], z * NY + frm, head).wait_recv()
    order = [8, 7, 9, 6, 10, 5, 11, 4, 12, 3, 13, 2, 14, 1, 15]
    for i in order:
        to = zp(i)
        start(remote(by_y.at[:, to], by_z.at[z], rz_s.at[to], rz_r.at[z], to * NY + y, head))
    by_z[z] = by_y[:, z]
    for i in reversed(order):
        frm = zp(i)
        remote(by_y.at[:, frm], by_z.at[frm], rz_s.at[frm], rz_r.at[frm], frm * NY + y, head).wait_recv()
    routed_ref[...] = by_z[...].reshape(SESS, 2 * CAP, HD)

    for copy in sends:
        copy.wait_send()
    for chunk in range(NZ):
        @pl.when(chunk // 2 != head)
        def _(chunk=chunk):
            remote(
                partial.at[chunk], received.at[x, c, 0],
                sum_s.at[chunk], sum_r.at[x, c, 0], seq, other,
            ).wait_send()


def project(store_hidden, owner_row, new_hidden, key_columns, value_columns):
    dma = pltpu.SemaphoreType.DMA
    vmem = pl.BlockSpec(memory_space=pltpu.VMEM)
    return pl.pallas_call(
        project_kernel,
        out_shape=(
            jax.ShapeDtypeStruct((SESS, 2 * CAP, HD), jnp.bfloat16),
            jax.ShapeDtypeStruct((2, HD, TURN), jnp.float32),
        ),
        in_specs=[vmem] * 5,
        out_specs=(vmem, vmem),
        scratch_shapes=[
            pltpu.VMEM((ROWS, CHIP_FEAT), jnp.bfloat16),
            pltpu.VMEM((2, 16, FEAT), jnp.bfloat16),
            pltpu.VMEM((NZ, NY, 16, CHIP_FEAT), jnp.bfloat16),
            pltpu.VMEM((NZ, 64, ROWS), jnp.bfloat16),
            pltpu.VMEM((NX, 2, 2, 64, ROWS), jnp.bfloat16),
            pltpu.VMEM((2 * NX, 8, ROWS), jnp.float32),
            pltpu.VMEM((HIST, STORED), jnp.bfloat16),
            pltpu.VMEM((NY, NZ, 2 * CAP, HD), jnp.bfloat16),
            pltpu.VMEM((NY, NZ, 2 * CAP, HD), jnp.bfloat16),
            pltpu.VMEM((NZ, NY, 2 * CAP, HD), jnp.bfloat16),
            dma((2,)), dma((2,)),
            dma((2, 2, 9)), dma((2, 2, 9)),
            dma((18, 2, 2)), dma((18, 2, 2)),
            dma((NZ,)), dma((NX, 2, 2)),
            dma((2 * NX,)), dma((2 * NX,)),
            dma((NY,)), dma((NY,)),
            dma((NZ,)), dma((NZ,)),
        ],
        compiler_params=pltpu.CompilerParams(
            collective_id=0, has_side_effects=True, vmem_limit_bytes=48 * 1024 * 1024
        ),
        name="project_rows",
    )(store_hidden, owner_row, new_hidden, key_columns, value_columns)


def attend_kernel(
    turn_ref, rows_ref, fresh_ref, query_ref, cos_ref, sin_ref, out_ref, key_ref, value_ref
):
    def rotate(values, cosine, sine):
        return values * cosine + pltpu.roll(values, HD // 2, 1) * sine

    rows = rows_ref[...].astype(jnp.float32)
    sent_keys = rows[:, :CAP].reshape(HIST, HD)
    sent_values = rows[:, CAP:].reshape(HIST, HD)
    valid = jnp.abs(sent_keys) < EMPTY_TEST
    sent_keys = jnp.where(valid, sent_keys, 0.0).astype(jnp.bfloat16)
    marks = jnp.where(valid, 1.0, 0.0)
    row_at = lax.broadcasted_iota(jnp.int32, (HIST, HIST), 0)
    lane_at = lax.broadcasted_iota(jnp.int32, (HIST, HIST), 1)
    before = jnp.where(lane_at < row_at, 1.0, 0.0).astype(jnp.bfloat16)
    position = jnp.dot(before, marks.astype(jnp.bfloat16), preferred_element_type=jnp.float32)
    position = jnp.where(valid, position, -1.0).T[:1].astype(jnp.int32)
    place = jnp.where(row_at == position, 1.0, 0.0).astype(jnp.bfloat16)
    history = jnp.dot(
        place,
        jnp.concatenate([sent_keys, sent_values.astype(jnp.bfloat16)], axis=1),
        preferred_element_type=jnp.float32,
    )
    length = jnp.sum(marks[:, :1]).astype(jnp.int32)
    turn = turn_ref[0]

    key_ref[0, :HIST] = rotate(history[:, :HD], cos_ref[:HIST], sin_ref[:HIST]).astype(jnp.bfloat16)
    value_ref[0, :HIST] = history[:, HD:].astype(jnp.bfloat16)
    cosine = cos_ref[pl.ds(length, TURN), :]
    sine = sin_ref[pl.ds(length, TURN), :]
    live = lax.broadcasted_iota(jnp.int32, (TURN, HD), 0) < turn
    key_ref[0, HIST:] = jnp.where(live, rotate(fresh_ref[0].T, cosine, sine), 0.0).astype(jnp.bfloat16)
    value_ref[0, HIST:] = jnp.where(live, fresh_ref[1].T, 0.0).astype(jnp.bfloat16)

    keys = key_ref[0]
    values = value_ref[0]
    slot_at = lax.broadcasted_iota(jnp.int32, (TURN, CACHE), 0)
    cache_at = lax.broadcasted_iota(jnp.int32, (TURN, CACHE), 1)
    allowed = (cache_at < length) | ((cache_at >= HIST) & (cache_at - HIST <= slot_at))
    for group in range(QH // KVH):
        at = pl.ds(group * HD, HD)
        query = rotate(query_ref[:, at].astype(jnp.float32), cosine, sine).astype(jnp.bfloat16)
        scores = nt_dot(query, keys) * (1.0 / math.sqrt(HD))
        scores = jnp.where(allowed, scores, -jnp.inf)
        exponent = jnp.exp(scores - jnp.max(scores, axis=1, keepdims=True))
        weights = (exponent / jnp.sum(exponent, axis=1, keepdims=True)).astype(jnp.bfloat16)
        result = jnp.dot(weights, values, preferred_element_type=jnp.float32)
        out_ref[:, at] = jnp.where(live, result, 0.0).astype(jnp.bfloat16)


def attend(turn_length, rows, fresh, queries):
    cosine, sine = rotation_tables()
    vmem = pl.BlockSpec(memory_space=pltpu.VMEM)
    return pl.pallas_call(
        attend_kernel,
        out_shape=(
            jax.ShapeDtypeStruct((TURN, QH // KVH * HD), jnp.bfloat16),
            jax.ShapeDtypeStruct((1, CACHE, HD), jnp.bfloat16),
            jax.ShapeDtypeStruct((1, CACHE, HD), jnp.bfloat16),
        ),
        in_specs=[pl.BlockSpec(memory_space=pltpu.SMEM)] + [vmem] * 5,
        out_specs=(vmem, vmem, vmem),
        compiler_params=pltpu.CompilerParams(vmem_limit_bytes=48 * 1024 * 1024),
        name="attend_turn",
    )(turn_length, rows, fresh, queries, jnp.asarray(cosine), jnp.asarray(sine))


def local(store_hidden, owner_map, new_hidden, new_lengths, queries, key_weight, value_weight):
    rows, fresh = project(
        store_hidden, owner_map.reshape(1, STORED), new_hidden, key_weight.T, value_weight.T
    )
    return attend(new_lengths, rows, fresh, queries)


def solution(mesh):
    placed = (
        P("seq", "head"),
        P("seq", None),
        P("seq", "head"),
        P("seq"),
        P("seq", "head"),
        P("head", "seq"),
        P("head", "seq"),
    )
    return jax.shard_map(
        local,
        mesh=mesh,
        in_specs=placed,
        out_specs=(P("seq", "head"), P("seq", None, "head"), P("seq", None, "head")),
        check_vma=False,
    )
```

time: 365 us -> 93.7 us (0.26)
  waiting for transfers between devices: 226 us -> 0 us
  Pallas kernels: 0 us -> 86 us
  local copies, waits for them, and re-layouts: 45.1 us -> 5.13 us
  starting transfers between devices: 33.9 us -> 0 us
  blocking collectives: 21.5 us -> 0 us
  between operations: 14.7 us -> 1.32 us
  other arithmetic: 11.9 us -> 0 us
  matrix products: 9.96 us -> 0 us
    all_gather x2 -> x0, waiting for transfers between devices: 152 us -> none  [the longest x1 133 us: local(): lax.all_gather(value_weight, 'seq', axis=1, tiled=True)]
    pallas_call x0 -> x2, Pallas kernels: none -> 86 us  [the longest x1 81.1 us: project(): pl.pallas_call(project_kernel, out_shape=(jax.ShapeDtypeStruct((SESS, 2 *...]
    all_to_all x2 -> x0, waiting for transfers between devices: 52.8 us -> none  [the longest x1 52.8 us: local(): lax.all_to_all(outgoing, 'seq', split_axis=0, concat_axis=0, tiled=True)]
    scatter x2 -> x0, local copies, waits for them, and re-layouts: 39.5 us -> none  [the longest x1 36.7 us: local(): outgoing = jnp.zeros((sessions, capacity, store_hidden.shape[1]), jnp.bfl...]
    all_to_all x2 -> x0, starting transfers between devices: 33.8 us -> none  [the longest x1 19.3 us: local(): lax.all_to_all(owner_counts[:, None], 'seq', split_axis=0, concat_axis=0,...]
    psum x1 -> x0, blocking collectives: 21.5 us -> none  [local(): totals = lax.psum(squares, 'head')]
    reduce_scatter x1 -> x0, waiting for transfers between devices: 19.9 us -> none  [local(): lax.psum_scatter(jnp.concatenate([key_term, value_term], axis=2).astype(j...]
    unnamed x2 -> x0, matrix products: 8.48 us -> none
  transfers between devices with their start and end apart: 5 -> 0, of which waited for: 4 -> 0; matrix products, arithmetic and copies ran while one was open for 15% -> 0% of each run, Pallas kernels for 0% -> 0%
where the time goes in v1:
time: 93.7 us; the launch traced here: 92.5 us
  Pallas kernels  86 us (92%)
  local copies, waits for them, and re-layouts  5.13 us (5%)
  between operations  1.32 us (1%)
    pallas_call x1, Pallas kernels, project(): pl.pallas_call(project_kernel, out_shape=(jax.ShapeDtypeStruct((SESS, 2 *...  81.1 us
    unnamed x16, local copies, waits for them, and re-layouts  5.13 us
    pallas_call x1, Pallas kernels, attend(): pl.pallas_call(attend_kernel, out_shape=(jax.ShapeDtypeStruct((TURN, QH /...  4.95 us

profile of v1, /device:TPU:1, one launch (start us, length us, event | category | flops | bytes accessed | tf_op | source)
XLA Modules:
  0.0 92.5 jit_solution(17040049836066361916)
XLA Ops:
  1.3 0.0 copy-start.7
  1.3 0.7 copy-done.7
  2.0 0.0 copy-start
  2.0 1.0 %copy-done = bf16[256,1024]{1,0:T(8,128)(2,1)S(1)} copy-done((bf16[256,1024]{1,0:T(8,128)(2,1)S(1)}, bf16[256,1024]{1,0:T(8,128)(2,1)}, u32[]{:S(2)}) %copy-start) | copy-done | bytes 524312
  3.0 0.0 copy-start.4
  3.0 0.9 %copy-done.4 = bf16[128,1024]{1,0:T(8,128)(2,1)S(1)} copy-done((bf16[128,1024]{1,0:T(8,128)(2,1)S(1)}, bf16[128,1024]{1,0:T(8,128)(2,1)}, u32[]{:S(2)}) %copy-start.4) | copy-done | bytes 262168
  4.0 0.0 copy-start.5
  4.0 0.8 copy-done.5
  4.7 0.0 copy-start.6
  4.7 0.8 copy-done.6
  5.5 0.0 copy-start.1
  5.5 0.0 copy-start.2
  5.5 81.1 %project_rows.1 = (bf16[64,16,128]{2,1,0:T(8,128)(2,1)S(1)}, f32[2,128,128]{2,1,0:T(8,128)S(1)}) custom-call(bf16[256,1024]{1,0:T(8,128)(2,1)S(1)} %copy-done, s32[1,256]{1,0:T(1,128)S(1)} %bitcast.5, bf16[128,1024]{1,0:T(8,128)(2,1)S(1)} %copy-done.4, bf16[16,1024]{1,0:T(8,128)(2,1)S(1)} %bitcast.3, bf16[16,1024]{1,0:T(8,128)(2,1)S(1)} %bitcast.4), custom_call_target="tpu_custom_call" | custom-call | tf_op jit(solution)/shard_map/project_rows/pallas_call | solution.py:300
  86.5 0.0 copy-done.1
  86.5 0.0 copy-done.2
  86.6 0.0 copy-start.3
  86.6 0.9 %copy-done.3 = bf16[128,1024]{1,0:T(8,128)(2,1)S(1)} copy-done((bf16[128,1024]{1,0:T(8,128)(2,1)S(1)}, bf16[128,1024]{1,0:T(8,128)(2,1)}, u32[]{:S(2)}) %copy-start.3) | copy-done | bytes 262168
  87.5 5.0 %attend_turn.1 = (bf16[128,1024]{1,0:T(8,128)(2,1)}, bf16[1,640,128]{2,1,0:T(8,128)(2,1)}, bf16[1,640,128]{2,1,0:T(8,128)(2,1)}) custom-call(s32[1]{0:T(128)S(6)} %copy.12.turn_ref, bf16[64,16,128]{2,1,0:T(8,128)(2,1)S(1)} %get-tuple-element.5.rows_ref, f32[2,128,128]{2,1,0:T(8,128)S(1)} %get-tuple-element.6.fresh_ref, bf16[128,1024]{1,0:T(8,128)(2,1)S(1)} %copy-done.3, ...), custom_call_target="tpu_custom_call" | custom-call | tf_op jit(solution)/shard_map/attend_turn/pallas_call | solution.py:387
Async XLA Ops:
  1.3 0.7 copy-start.7
  2.0 1.0 %copy-start = (bf16[256,1024]{1,0:T(8,128)(2,1)S(1)}, bf16[256,1024]{1,0:T(8,128)(2,1)}, u32[]{:S(2)}) copy-start(bf16[256,1024]{1,0:T(8,128)(2,1)} %store_ref.1) | copy-start | bytes 1572868
  3.0 0.9 %copy-start.4 = (bf16[128,1024]{1,0:T(8,128)(2,1)S(1)}, bf16[128,1024]{1,0:T(8,128)(2,1)}, u32[]{:S(2)}) copy-start(bf16[128,1024]{1,0:T(8,128)(2,1)} %new_ref.1) | copy-start | bytes 786436
  4.0 0.8 copy-start.5
  4.7 0.8 copy-start.6
  5.5 81.1 %copy-start.1 = (f32[640,128]{1,0:T(8,128)S(1)}, f32[640,128]{1,0:T(8,128)}, u32[]{:S(2)}) copy-start(f32[640,128]{1,0:T(8,128)} %constant.5.clone.sin_ref) | copy-start | bytes 983044
  5.5 81.1 %copy-start.2 = (f32[640,128]{1,0:T(8,128)S(1)}, f32[640,128]{1,0:T(8,128)}, u32[]{:S(2)}) copy-start(f32[640,128]{1,0:T(8,128)} %constant.4.clone.cos_ref) | copy-start | bytes 983044
  86.6 1.0 %copy-start.3 = (bf16[128,1024]{1,0:T(8,128)(2,1)S(1)}, bf16[128,1024]{1,0:T(8,128)(2,1)}, u32[]{:S(2)}) copy-start(bf16[128,1024]{1,0:T(8,128)(2,1)} %query_ref.1) | copy-start | bytes 786436

commit v2 on v1

--- a/solution.py
+++ b/solution.py
@@ -56,8 +56,8 @@
 def project_kernel(
     store_ref, owner_ref, new_ref, kw_ref, vw_ref,
     routed_ref, fresh_ref,
-    xs, wl, gathered, partial, received, squares, onehot, outgoing, by_y, by_z,
-    core_s, core_r, z_s, z_r, y_s, y_r, sum_s, sum_r, sq_s, sq_r, ry_s, ry_r, rz_s, rz_r,
+    xs, owners, gathered, partial, received, squares, onehot, empties, outgoing, by_y, by_z,
+    in_s, core_s, core_r, z_s, z_r, y_s, y_r, sum_s, sum_r, sq_s, sq_r, ry_s, ry_r, rz_s, rz_r,
 ):
     seq = lax.axis_index("seq")
     head = lax.axis_index("head")
@@ -84,71 +84,111 @@
         sends.append(copy)
 
     barrier = pltpu.get_barrier_semaphore()
-    peers = [(seq, lax.rem(head + i, 2 * NX)) for i in range(1, 2 * NX)]
-    peers += [(z * NY + yp(i), head) for i in range(1, NY)]
-    peers += [(zp(i) * NY + y, head) for i in range(1, NZ)]
+    peers = [(z * NY + yp(i), head) for i in (1, -1)]
+    peers += [(zp(i) * NY + y, head) for i in (1, -1)]
+    peers += [(seq, lax.rem(head + i, 2 * NX)) for i in range(1, 2 * NX)]
     for peer in peers:
         pl.semaphore_signal(barrier, inc=1, device_id=peer, device_id_type=MESH)
 
     own = pl.ds(pl.multiple_of(c * FEAT, FEAT), FEAT)
     theirs = pl.ds(pl.multiple_of((1 - c) * FEAT, FEAT), FEAT)
-    wl[0] = kw_ref[...]
-    wl[1] = vw_ref[...]
-    gathered[z, y, :, own] = wl[c]
-    xs[:STORED, own] = store_ref[...]
-    xs[STORED:, own] = new_ref[...]
+    mine = gathered.at[z, y, :, own]
+
+    def own_weights(ref):
+        return pltpu.make_async_copy(ref, mine, in_s.at[0])
+
+    def their_weights(ref):
+        return remote(ref, mine, core_s.at[0], core_r.at[0], seq, other)
+
+    @pl.when(c == 0)
+    def _():
+        own_weights(kw_ref).start()
+
+    @pl.when(c == 1)
+    def _():
+        own_weights(vw_ref).start()
+
+    store_in = pltpu.make_async_copy(store_ref, xs.at[:STORED, own], in_s.at[1])
+    new_in = pltpu.make_async_copy(new_ref, xs.at[STORED:, own], in_s.at[2])
+    owner_in = pltpu.make_async_copy(owner_ref, owners, in_s.at[3])
+    for copy in (store_in, new_in, owner_in):
+        copy.start()
     pl.semaphore_wait(barrier, len(peers))
 
-    start(remote(wl.at[1 - c], gathered.at[z, y, :, own], core_s.at[0], core_r.at[0], seq, other))
-    start(remote(xs.at[:, own], xs.at[:, own], core_s.at[1], core_r.at[1], seq, other))
+    @pl.when(c == 0)
+    def _():
+        their_weights(vw_ref).start()
+
+    @pl.when(c == 1)
+    def _():
+        their_weights(kw_ref).start()
+
+    start(remote(store_ref, xs.at[:STORED, own], core_s.at[1], core_r.at[1], seq, other))
+    start(remote(new_ref, xs.at[STORED:, own], core_s.at[2], core_r.at[2], seq, other))
+    own_weights(kw_ref).wait()
     remote(
-        wl.at[1 - c], gathered.at[z, y, :, theirs], core_s.at[0], core_r.at[0], seq, other
+        kw_ref, gathered.at[z, y, :, theirs], core_s.at[0], core_r.at[0], seq, other
     ).wait_recv()
 
-    def z_region(flow, chunk):
-        if flow == 0:
-            return gathered.at[chunk, y, :, :SPLIT]
-        return gathered.at[chunk, :, :, SPLIT:]
-
-    def z_target(d):
-        return zp(1 if d == 0 else -1) * NY + y
+    flows = [
+        (0, 0, SPLIT, 0, 0),
+        (0, SPLIT, CHIP_FEAT, 0, 0),
+        (-1, SPLIT, CHIP_FEAT, 1, 1),
+        (1, SPLIT, CHIP_FEAT, 1, 1),
+        (2, SPLIT, CHIP_FEAT, 1, 2),
+    ]
+    far = NZ // 2
 
     def z_chunk(d, t):
         return zp(-t if d == 0 else t)
 
-    def z_send(flow, d, t):
-        region = z_region(flow, z_chunk(d, t - 1))
-        start(remote(region, region, z_s.at[flow, d, t], z_r.at[flow, d, t], z_target(d), head))
-
-    def z_wait(flow, d, t):
-        region = z_region(flow, z_chunk(d, t))
-        remote(region, region, z_s.at[flow, d, t], z_r.at[flow, d, t], z_target(d), head).wait_recv()
+    def z_copy(flow, d, t, chunk):
+        delta, lo, hi = flows[flow][:3]
+        region = gathered.at[chunk, yp(delta), :, lo:hi]
+        return remote(
+            region, region, z_s.at[flow, d, t], z_r.at[flow, d, t],
+            zp(1 if d == 0 else -1) * NY + y, head,
+        )
 
     def z_has(flow, d, t):
-        return t < NZ // 2 or (t == NZ // 2 and flow == d)
-
-    def y_target(d):
-        return z * NY + yp(1 if d == 0 else -1)
+        return t < far or (t == far and flows[flow][3] == d)
+
+    def z_first(flow):
+        for d in (0, 1):
+            start(z_copy(flow, d, 1, z))
+
+    def z_pass(flow, t):
+        for d in (0, 1):
+            if z_has(flow, d, t):
+                chunk = z_chunk(d, t)
+                z_copy(flow, d, t, chunk).wait_recv()
+                if z_has(flow, d, t + 1):
+                    start(z_copy(flow, d, t + 1, chunk))
 
     def y_copy(index, chunk, lo, hi, stage, d, delta):
         region = gathered.at[chunk, yp(delta), :, lo:hi]
         return remote(
-            region, region, y_s.at[index, stage, d], y_r.at[index, stage, d], y_target(d), head
+            region, region, y_s.at[index, stage, d], y_r.at[index, stage, d],
+            z * NY + yp(1 if d == 0 else -1), head,
         )
 
     def y_one(index, chunk, lo, hi):
         for d in (0, 1):
             start(y_copy(index, chunk, lo, hi, 0, d, 0))
 
-    def y_two(index, chunk, lo, hi):
-        mid = (lo + hi) // 2
-        y_copy(index, chunk, lo, hi, 0, 0, -1).wait_recv()
-        start(y_copy(index, chunk, lo, mid, 1, 0, -1))
-        y_copy(index, chunk, lo, hi, 0, 1, 1).wait_recv()
-        start(y_copy(index, chunk, mid, hi, 1, 1, 1))
+    def half_way(lo, hi):
+        return lo + (hi - lo) // 256 * 128
+
+    def y_two(index, chunk, lo, hi, d):
+        mid = half_way(lo, hi)
+        y_copy(index, chunk, lo, hi, 0, d, -1 if d == 0 else 1).wait_recv()
+        if d == 0:
+            start(y_copy(index, chunk, lo, mid, 1, 0, -1))
+        else:
+            start(y_copy(index, chunk, mid, hi, 1, 1, 1))
 
     def y_end(index, chunk, lo, hi):
-        mid = (lo + hi) // 2
+        mid = half_way(lo, hi)
         y_copy(index, chunk, lo, mid, 1, 0, 2).wait_recv()
         y_copy(index, chunk, mid, hi, 1, 1, 2).wait_recv()
 
@@ -157,42 +197,44 @@
             return [(0, z)]
         return [(2 * t + d, z_chunk(d, t)) for d in (0, 1) if z_has(0, d, t)]
 
-    for d in (0, 1):
-        z_send(0, d, 1)
-    y_one(1, z, SPLIT, CHIP_FEAT)
-    y_one(0, z, 0, SPLIT)
-
-    ones = jnp.ones((8, 256), jnp.bfloat16)
-    total = jnp.zeros((8, ROWS), jnp.float32)
-    for piece in range(FEAT // 256):
-        at = pl.ds(piece * 256, 256)
-        block = jnp.concatenate([store_ref[:, at], new_ref[:, at]], axis=0).astype(jnp.float32)
-        square = block * block
-        high = square.astype(jnp.bfloat16)
-        low = (square - high.astype(jnp.float32)).astype(jnp.bfloat16)
-        total += nt_dot(ones, high) + nt_dot(ones, low)
-    squares[head] = total
-    for i in range(1, 2 * NX):
-        to = lax.rem(head + i, 2 * NX)
-        start(remote(squares.at[head], squares.at[head], sq_s.at[to], sq_r.at[head], seq, to))
-
-    y_two(1, z, SPLIT, CHIP_FEAT)
-
-    owner_row = owner_ref[...]
-    owner_lanes = jnp.broadcast_to(owner_row.astype(jnp.float32), (STORED, STORED))
-    earlier = lax.broadcasted_iota(jnp.int32, (STORED, STORED), 0) < lax.broadcasted_iota(
-        jnp.int32, (STORED, STORED), 1
-    )
-    same = jnp.where(earlier & (owner_lanes.T == owner_lanes), 1.0, 0.0)
-    rank = jnp.sum(same, axis=0, keepdims=True).astype(jnp.int32)
-    owner_z = lax.shift_right_logical(owner_row, 2)
-    owner_y = lax.bitwise_and(owner_row, 3)
-    slot = (owner_y * NZ + owner_z) * CAP + rank
-    onehot[...] = jnp.where(
-        lax.broadcasted_iota(jnp.int32, (HIST, STORED), 0) == slot, 1.0, 0.0
-    ).astype(jnp.bfloat16)
-
-    remote(xs.at[:, theirs], xs.at[:, theirs], core_s.at[1], core_r.at[1], seq, other).wait_recv()
+    def sum_squares():
+        store_in.wait()
+        new_in.wait()
+        ones = jnp.ones((8, 256), jnp.bfloat16)
+        total = jnp.zeros((8, ROWS), jnp.float32)
+        for piece in range(FEAT // 256):
+            at = pl.ds(pl.multiple_of(c * FEAT + piece * 256, 256), 256)
+            block = xs[:, at].astype(jnp.float32)
+            square = block * block
+            high = square.astype(jnp.bfloat16)
+            low = (square - high.astype(jnp.float32)).astype(jnp.bfloat16)
+            total += nt_dot(ones, high) + nt_dot(ones, low)
+        squares[head] = total
+        for i in range(1, 2 * NX):
+            to = lax.rem(head + i, 2 * NX)
+            start(remote(squares.at[head], squares.at[head], sq_s.at[to], sq_r.at[head], seq, to))
+
+    def find_slots():
+        owner_in.wait()
+        owner_row = owners[...]
+        owner_lanes = jnp.broadcast_to(owner_row.astype(jnp.float32), (STORED, STORED))
+        earlier = lax.broadcasted_iota(jnp.int32, (STORED, STORED), 0) < lax.broadcasted_iota(
+            jnp.int32, (STORED, STORED), 1
+        )
+        same = jnp.where(earlier & (owner_lanes.T == owner_lanes), 1.0, 0.0)
+        rank = jnp.sum(same, axis=0, keepdims=True).astype(jnp.int32)
+        owner_z = lax.shift_right_logical(owner_row, 2)
+        owner_y = lax.bitwise_and(owner_row, 3)
+        slot = (owner_y * NZ + owner_z) * CAP + rank
+        hot = jnp.where(lax.broadcasted_iota(jnp.int32, (HIST, STORED), 0) == slot, 1.0, 0.0)
+        onehot[...] = hot.astype(jnp.bfloat16)
+        filled = jnp.sum(hot, axis=1, keepdims=True)
+        empties[...] = jnp.broadcast_to((1.0 - filled) * EMPTY, (HIST, HD))
+
+    def take_rows():
+        for i, rows in ((1, slice(0, STORED)), (2, slice(STORED, ROWS))):
+            region = xs.at[rows, theirs]
+            remote(region, region, core_s.at[i], core_r.at[i], seq, other).wait_recv()
 
     def send_sum(chunk):
         to = lax.div(chunk, 2)
@@ -211,28 +253,37 @@
                 sum_s.at[chunk], sum_r.at[x, c, half], seq, to,
             ).start()
 
-    last = NZ // 2
-    for s in range(1, last + 3):
-        if s <= last:
-            for d in (0, 1):
-                if z_has(0, d, s):
-                    z_wait(0, d, s)
-                    if z_has(0, d, s + 1):
-                        z_send(0, d, s + 1)
-                    y_one(2 * s + d, z_chunk(d, s), 0, SPLIT)
+    z_first(0)
+    z_first(1)
+    y_one(1, z, SPLIT, CHIP_FEAT)
+    y_one(0, z, 0, SPLIT)
+    for d in (0, 1):
+        y_two(1, z, SPLIT, CHIP_FEAT, d)
+        z_first(2 + d)
+
+    for s in range(1, far + 3):
+        if s <= far:
+            z_pass(0, s)
+            z_pass(1, s)
+            for index, chunk in chunks_of(s):
+                y_one(index, chunk, 0, SPLIT)
+        if 1 <= s - 1 <= far:
+            z_pass(2, s - 1)
+            z_pass(3, s - 1)
         if s == 1:
             y_end(1, z, SPLIT, CHIP_FEAT)
-            for d in (0, 1):
-                z_send(1, d, 1)
-        elif s - 1 <= last:
-            for d in (0, 1):
-                if z_has(1, d, s - 1):
-                    z_wait(1, d, s - 1)
-                    if z_has(1, d, s):
-                        z_send(1, d, s)
-        if s - 1 <= last:
+            z_first(4)
+        elif 1 <= s - 2 <= far:
+            z_pass(4, s - 2)
+        if s == 1:
+            sum_squares()
+        if s - 1 <= far:
             for index, chunk in chunks_of(s - 1):
-                y_two(index, chunk, 0, SPLIT)
+                for d in (0, 1):
+                    y_two(index, chunk, 0, SPLIT, d)
+        if s == 2:
+            find_slots()
+            take_rows()
         if s >= 2:
             for index, chunk in chunks_of(s - 2):
                 y_end(index, chunk, 0, SPLIT)
@@ -259,8 +310,7 @@
         scaled = summed * scale
         fresh_ref[kind] = scaled[:, STORED:]
         kinds.append(nt_dot(onehot[...], scaled[:, :STORED].astype(jnp.bfloat16)))
-    filled = jnp.sum(onehot[...].astype(jnp.float32), axis=1, keepdims=True)
-    keys = kinds[0] + (1.0 - filled) * EMPTY
+    keys = kinds[0] + empties[...]
     slots = jnp.concatenate(
         [keys.reshape(SESS, CAP, HD), kinds[1].reshape(SESS, CAP, HD)], axis=1
     )
@@ -283,6 +333,7 @@
         remote(by_y.at[:, frm], by_z.at[frm], rz_s.at[frm], rz_r.at[frm], frm * NY + y, head).wait_recv()
     routed_ref[...] = by_z[...].reshape(SESS, 2 * CAP, HD)
 
+    their_weights(kw_ref).wait_send()
     for copy in sends:
         copy.wait_send()
     for chunk in range(NZ):
@@ -303,21 +354,23 @@
             jax.ShapeDtypeStruct((SESS, 2 * CAP, HD), jnp.bfloat16),
             jax.ShapeDtypeStruct((2, HD, TURN), jnp.float32),
         ),
-        in_specs=[vmem] * 5,
+        in_specs=[pl.BlockSpec(memory_space=pltpu.HBM)] * 5,
         out_specs=(vmem, vmem),
         scratch_shapes=[
             pltpu.VMEM((ROWS, CHIP_FEAT), jnp.bfloat16),
-            pltpu.VMEM((2, 16, FEAT), jnp.bfloat16),
+            pltpu.VMEM((1, STORED), jnp.int32),
             pltpu.VMEM((NZ, NY, 16, CHIP_FEAT), jnp.bfloat16),
             pltpu.VMEM((NZ, 64, ROWS), jnp.bfloat16),
             pltpu.VMEM((NX, 2, 2, 64, ROWS), jnp.bfloat16),
             pltpu.VMEM((2 * NX, 8, ROWS), jnp.float32),
             pltpu.VMEM((HIST, STORED), jnp.bfloat16),
+            pltpu.VMEM((HIST, HD), jnp.float32),
             pltpu.VMEM((NY, NZ, 2 * CAP, HD), jnp.bfloat16),
             pltpu.VMEM((NY, NZ, 2 * CAP, HD), jnp.bfloat16),
             pltpu.VMEM((NZ, NY, 2 * CAP, HD), jnp.bfloat16),
-            dma((2,)), dma((2,)),
-            dma((2, 2, 9)), dma((2, 2, 9)),
+            dma((4,)),
+            dma((3,)), dma((3,)),
+            dma((5, 2, 9)), dma((5, 2, 9)),
             dma((18, 2, 2)), dma((18, 2, 2)),
             dma((NZ,)), dma((NX, 2, 2)),
             dma((2 * NX,)), dma((2 * NX,)),

time: 93.7 us -> 88.6 us (0.946)
  Pallas kernels: 86 us -> 81.8 us
    pallas_call x1, Pallas kernels: 81.1 us -> 76.8 us  [project(): pl.pallas_call(project_kernel, out_shape=(jax.ShapeDtypeStruct((SESS, 2 *...]
where the time goes in v2:
time: 88.6 us; the launch traced here: 88.2 us
  Pallas kernels  81.8 us (92%)
  local copies, waits for them, and re-layouts  5.13 us (6%)
  between operations  1.32 us (1%)
    pallas_call x1, Pallas kernels, project(): pl.pallas_call(project_kernel, out_shape=(jax.ShapeDtypeStruct((SESS, 2 *...  76.8 us
    unnamed x16, local copies, waits for them, and re-layouts  5.13 us
    pallas_call x1, Pallas kernels, attend(): pl.pallas_call(attend_kernel, out_shape=(jax.ShapeDtypeStruct((TURN, QH /...  4.96 us

profile of v2, /device:TPU:1, one launch (start us, length us, event | category | flops | bytes accessed | tf_op | source)
XLA Modules:
  0.0 88.2 jit_solution(3781606147885722192)
XLA Ops:
  1.3 0.0 copy-start.7
  1.3 0.7 copy-done.7
  2.0 0.0 copy-start
  2.0 1.0 %copy-done = bf16[256,1024]{1,0:T(8,128)(2,1)S(1)} copy-done((bf16[256,1024]{1,0:T(8,128)(2,1)S(1)}, bf16[256,1024]{1,0:T(8,128)(2,1)}, u32[]{:S(2)}) %copy-start) | copy-done | bytes 524312
  3.0 0.0 copy-start.4
  3.0 0.9 %copy-done.4 = bf16[128,1024]{1,0:T(8,128)(2,1)S(1)} copy-done((bf16[128,1024]{1,0:T(8,128)(2,1)S(1)}, bf16[128,1024]{1,0:T(8,128)(2,1)}, u32[]{:S(2)}) %copy-start.4) | copy-done | bytes 262168
  4.0 0.0 copy-start.5
  4.0 0.8 copy-done.5
  4.7 0.0 copy-start.6
  4.7 0.8 copy-done.6
  5.5 0.0 copy-start.1
  5.5 0.0 copy-start.2
  5.5 76.8 %project_rows.1 = (bf16[64,16,128]{2,1,0:T(8,128)(2,1)S(1)}, f32[2,128,128]{2,1,0:T(8,128)S(1)}) custom-call(bf16[256,1024]{1,0:T(8,128)(2,1)S(1)} %copy-done, s32[1,256]{1,0:T(1,128)S(1)} %bitcast.5, bf16[128,1024]{1,0:T(8,128)(2,1)S(1)} %copy-done.4, bf16[16,1024]{1,0:T(8,128)(2,1)S(1)} %bitcast.3, bf16[16,1024]{1,0:T(8,128)(2,1)S(1)} %bitcast.4), custom_call_target="tpu_custom_call" | custom-call | tf_op jit(solution)/shard_map/project_rows/pallas_call | solution.py:351
  82.3 0.0 copy-done.1
  82.3 0.0 copy-done.2
  82.3 0.0 copy-start.3
  82.3 0.9 %copy-done.3 = bf16[128,1024]{1,0:T(8,128)(2,1)S(1)} copy-done((bf16[128,1024]{1,0:T(8,128)(2,1)S(1)}, bf16[128,1024]{1,0:T(8,128)(2,1)}, u32[]{:S(2)}) %copy-start.3) | copy-done | bytes 262168
  83.2 5.0 %attend_turn.1 = (bf16[128,1024]{1,0:T(8,128)(2,1)}, bf16[1,640,128]{2,1,0:T(8,128)(2,1)}, bf16[1,640,128]{2,1,0:T(8,128)(2,1)}) custom-call(s32[1]{0:T(128)S(6)} %copy.12.turn_ref, bf16[64,16,128]{2,1,0:T(8,128)(2,1)S(1)} %get-tuple-element.5.rows_ref, f32[2,128,128]{2,1,0:T(8,128)S(1)} %get-tuple-element.6.fresh_ref, bf16[128,1024]{1,0:T(8,128)(2,1)S(1)} %copy-done.3, ...), custom_call_target="tpu_custom_call" | custom-call | tf_op jit(solution)/shard_map/attend_turn/pallas_call | solution.py:440
Async XLA Ops:
  1.3 0.7 copy-start.7
  2.0 1.0 %copy-start = (bf16[256,1024]{1,0:T(8,128)(2,1)S(1)}, bf16[256,1024]{1,0:T(8,128)(2,1)}, u32[]{:S(2)}) copy-start(bf16[256,1024]{1,0:T(8,128)(2,1)} %store_ref.1) | copy-start | bytes 1572868
  3.0 0.9 %copy-start.4 = (bf16[128,1024]{1,0:T(8,128)(2,1)S(1)}, bf16[128,1024]{1,0:T(8,128)(2,1)}, u32[]{:S(2)}) copy-start(bf16[128,1024]{1,0:T(8,128)(2,1)} %new_ref.1) | copy-start | bytes 786436
  4.0 0.8 copy-start.5
  4.7 0.8 copy-start.6
  5.5 76.8 %copy-start.1 = (f32[640,128]{1,0:T(8,128)S(1)}, f32[640,128]{1,0:T(8,128)}, u32[]{:S(2)}) copy-start(f32[640,128]{1,0:T(8,128)} %constant.5.clone.sin_ref) | copy-start | bytes 983044
  5.5 76.8 %copy-start.2 = (f32[640,128]{1,0:T(8,128)S(1)}, f32[640,128]{1,0:T(8,128)}, u32[]{:S(2)}) copy-start(f32[640,128]{1,0:T(8,128)} %constant.4.clone.cos_ref) | copy-start | bytes 983044
  82.3 1.0 %copy-start.3 = (bf16[128,1024]{1,0:T(8,128)(2,1)S(1)}, bf16[128,1024]{1,0:T(8,128)(2,1)}, u32[]{:S(2)}) copy-start(bf16[128,1024]{1,0:T(8,128)(2,1)} %query_ref.1) | copy-start | bytes 786436

commit v3 on v2

v3 whole, which is shorter than its diff:
```python
import functools
import math

import jax
import jax.numpy as jnp
import numpy as np
from jax import lax
from jax.experimental import pallas as pl
from jax.experimental.pallas import tpu as pltpu
from jax.sharding import PartitionSpec as P

D = 8192
QH = 64
KVH = 8
HD = 128
NZ = 16
NY = 4
NX = 4
STORED = 256
TURN = 128
ROWS = STORED + TURN
CAP = 8
SESS = NZ * NY
HIST = SESS * CAP
CACHE = HIST + TURN
FEAT = D // (2 * NX)
CHIP_FEAT = 2 * FEAT
SPLIT = 1664
LAG1 = 2.7
LAG2 = 5.4
EMPTY = float(2.0**100)
EMPTY_TEST = float(2.0**50)
MESH = pl.DeviceIdType.MESH
rope_base = 500000.0


def rotation_tables():
    half_index = np.arange(HD // 2, dtype=np.float64)
    inverse = 1.0 / np.power(rope_base, 2.0 * half_index / HD)
    wavelength = 2.0 * np.pi / inverse
    smooth = (8192.0 / wavelength - 1.0) / 3.0
    mixed = (1.0 - smooth) * inverse / 8.0 + smooth * inverse
    frequency = np.where(
        wavelength < 2048.0, inverse, np.where(wavelength > 8192.0, inverse / 8.0, mixed)
    )
    angles = np.arange(CACHE, dtype=np.float64)[:, None] * frequency[None, :]
    cosine, sine = np.cos(angles), np.sin(angles)
    return (
        np.concatenate([cosine, cosine], axis=1).astype(np.float32),
        np.concatenate([-sine, sine], axis=1).astype(np.float32),
    )


def nt_dot(a, b):
    return lax.dot_general(a, b, (((1,), (1,)), ((), ())), preferred_element_type=jnp.float32)


def project_kernel(
    store_ref, owner_ref, new_ref, kw_ref, vw_ref,
    routed_ref, fresh_ref,
    xs, owners, gathered, partial, received, squares, onehot, empties, fresh, outgoing, by_y, by_z,
    in_s, out_s, core_s, core_r, z_s, z_r, y_s, y_r, sum_s, sum_r, sq_s, sq_r, ry_s, ry_r, rz_s, rz_r,
):
    seq = lax.axis_index("seq")
    head = lax.axis_index("head")
    z, y = lax.div(seq, NY), lax.rem(seq, NY)
    x, c = lax.div(head, 2), lax.rem(head, 2)
    other = head + 1 - 2 * c

    def zp(delta):
        return lax.rem(z + delta + NZ, NZ)

    def yp(delta):
        return lax.rem(y + delta + NY, NY)

    def remote(src, dst, send_sem, recv_sem, to_seq, to_head):
        return pltpu.make_async_remote_copy(
            src_ref=src, dst_ref=dst, send_sem=send_sem, recv_sem=recv_sem,
            device_id=(to_seq, to_head), device_id_type=MESH,
        )

    clock = [0.0]
    sends = []

    def start(copy):
        copy.start()
        sends.append((clock[0], copy))

    def drain(age):
        while sends and sends[0][0] <= clock[0] - age:
            sends.pop(0)[1].wait_send()

    barrier = pltpu.get_barrier_semaphore()
    peers = [(z * NY + yp(i), head) for i in (1, -1)]
    peers += [(zp(i) * NY + y, head) for i in (1, -1)]
    peers += [(seq, lax.rem(head + i, 2 * NX)) for i in range(1, 2 * NX)]
    for peer in peers:
        pl.semaphore_signal(barrier, inc=1, device_id=peer, device_id_type=MESH)

    own = pl.ds(pl.multiple_of(c * FEAT, FEAT), FEAT)
    theirs = pl.ds(pl.multiple_of((1 - c) * FEAT, FEAT), FEAT)
    mine = gathered.at[z, 0, :, own]

    def own_weights(ref):
        return pltpu.make_async_copy(ref, mine, in_s.at[0])

    def their_weights(ref):
        return remote(ref, mine, core_s.at[0], core_r.at[0], seq, other)

    @pl.when(c == 0)
    def _():
        own_weights(kw_ref).start()

    @pl.when(c == 1)
    def _():
        own_weights(vw_ref).start()

    store_in = pltpu.make_async_copy(store_ref, xs.at[:STORED, own], in_s.at[1])
    new_in = pltpu.make_async_copy(new_ref, xs.at[STORED:, own], in_s.at[2])
    owner_in = pltpu.make_async_copy(owner_ref, owners, in_s.at[3])
    for copy in (store_in, new_in, owner_in):
        copy.start()
    pl.semaphore_wait(barrier, len(peers))

    @pl.when(c == 0)
    def _():
        their_weights(vw_ref).start()

    @pl.when(c == 1)
    def _():
        their_weights(kw_ref).start()

    own_weights(kw_ref).wait()
    remote(
        kw_ref, gathered.at[z, 0, :, theirs], core_s.at[0], core_r.at[0], seq, other
    ).wait_recv()

    def z_region(way, chunk):
        if way == 0:
            return gathered.at[chunk, 0]
        return gathered.at[chunk, 1:, :, SPLIT:]

    def z_send(way, m, step):
        region = z_region(way, zp(-m))
        at = m + step + NZ // 2
        start(remote(region, region, z_s.at[way, at], z_r.at[way, at], zp(step) * NY + y, head))

    def z_take(way, m):
        region = z_region(way, zp(-m))
        at = m + NZ // 2
        remote(region, region, z_s.at[way, at], z_r.at[way, at], seq, head).wait_recv()

    def onward(way, m):
        if m == 0:
            return [1, -1]
        sign = 1 if m > 0 else -1
        last = NZ // 2 if sign == (1 if way == 0 else -1) else NZ // 2 - 1
        return [sign] if abs(m) < last else []

    def half_way(lo, hi):
        return lo + (hi - lo) // 256 * 128

    def y_piece(index, stage, d, src, dst):
        return remote(
            src, dst, y_s.at[index, stage, d], y_r.at[index, stage, d],
            z * NY + yp(1 if d == 0 else -1), head,
        )

    def y_one(index, chunk, lo, hi):
        for d in (0, 1):
            start(y_piece(
                index, 0, d, gathered.at[chunk, 0, :, lo:hi], gathered.at[chunk, 3 - 2 * d, :, lo:hi]
            ))

    def y_two(index, chunk, lo, hi):
        mid = half_way(lo, hi)
        for d in (0, 1):
            whole = gathered.at[chunk, 3 - 2 * d, :, lo:hi]
            y_piece(index, 0, d, whole, whole).wait_recv()
            part = slice(lo, mid) if d == 0 else slice(mid, hi)
            start(y_piece(
                index, 1, d, gathered.at[chunk, 3 - 2 * d, :, part], gathered.at[chunk, 2, :, part]
            ))

    def y_end(index, chunk, lo, hi):
        mid = half_way(lo, hi)
        for d in (0, 1):
            region = gathered.at[chunk, 2, :, lo:mid] if d == 0 else gathered.at[chunk, 2, :, mid:hi]
            y_piece(index, 1, d, region, region).wait_recv()

    def sum_squares():
        store_in.wait()
        new_in.wait()
        ones = jnp.ones((8, 256), jnp.bfloat16)
        total = jnp.zeros((8, ROWS), jnp.float32)
        for piece in range(FEAT // 256):
            at = pl.ds(pl.multiple_of(c * FEAT + piece * 256, 256), 256)
            block = xs[:, at].astype(jnp.float32)
            square = block * block
            high = square.astype(jnp.bfloat16)
            low = (square - high.astype(jnp.float32)).astype(jnp.bfloat16)
            total += nt_dot(ones, high) + nt_dot(ones, low)
        squares[head] = total
        for i in range(1, 2 * NX):
            to = lax.rem(head + i, 2 * NX)
            start(remote(squares.at[head], squares.at[head], sq_s.at[to], sq_r.at[head], seq, to))

    def find_slots():
        owner_in.wait()
        owner_row = owners[...]
        owner_lanes = jnp.broadcast_to(owner_row.astype(jnp.float32), (STORED, STORED))
        earlier = lax.broadcasted_iota(jnp.int32, (STORED, STORED), 0) < lax.broadcasted_iota(
            jnp.int32, (STORED, STORED), 1
        )
        same = jnp.where(earlier & (owner_lanes.T == owner_lanes), 1.0, 0.0)
        rank = jnp.sum(same, axis=0, keepdims=True).astype(jnp.int32)
        owner_z = lax.shift_right_logical(owner_row, 2)
        owner_y = lax.bitwise_and(owner_row, 3)
        slot = (owner_y * NZ + owner_z) * CAP + rank
        hot = jnp.where(lax.broadcasted_iota(jnp.int32, (HIST, STORED), 0) == slot, 1.0, 0.0)
        onehot[...] = hot.astype(jnp.bfloat16)
        filled = jnp.sum(hot, axis=1, keepdims=True)
        empties[...] = jnp.broadcast_to((1.0 - filled) * EMPTY, (HIST, HD))

    def send_rows():
        start(remote(store_ref, xs.at[:STORED, own], core_s.at[1], core_r.at[1], seq, other))
        start(remote(new_ref, xs.at[STORED:, own], core_s.at[2], core_r.at[2], seq, other))

    def take_rows():
        for i, rows in ((1, slice(0, STORED)), (2, slice(STORED, ROWS))):
            region = xs.at[rows, theirs]
            remote(region, region, core_s.at[i], core_r.at[i], seq, other).wait_recv()

    def send_sum(chunk):
        to = lax.div(chunk, 2)
        half = lax.rem(chunk, 2)
        result = nt_dot(gathered[chunk].reshape(4 * 16, CHIP_FEAT), xs[...]).astype(jnp.bfloat16)
        for r in range(NY):
            partial[chunk, yp(r)] = result[r * 16 : (r + 1) * 16]

        @pl.when(to == head)
        def _():
            received[x, c, half] = partial[chunk]

        @pl.when(to != head)
        def _():
            remote(
                partial.at[chunk], received.at[x, c, half],
                sum_s.at[chunk], sum_r.at[x, c, half], seq, to,
            ).start()

    arrives = {0: 0.0}
    todo = [0]
    while todo:
        m = todo.pop(0)
        for step in onward(0, m):
            arrives[m + step] = arrives[m] + 2.6
            todo.append(m + step)
    events = []
    for m, at in sorted(arrives.items(), key=lambda item: (item[1], item[0])):
        twin = m if abs(m) != NZ // 2 else -m
        if m != 0:
            events.append((at, 0, m))
            events.append((at + 5.3, 1, twin))
        events.append((at + LAG1, 2, m))
        events.append((at + LAG2, 3, m))
    events.append((2.4, 4, 0))
    events.append((5.0, 5, 0))
    events.append((3.0, 6, 0))
    events.append((5.1, 7, 0))
    events.append((5.2, 8, 0))

    for step in onward(0, 0):
        z_send(0, 0, step)
    y_one(17, z, SPLIT, CHIP_FEAT)
    send_rows()
    y_one(8, z, 0, SPLIT)
    for at, kind, m in sorted(events):
        clock[0] = at
        drain(6.0)
        chunk = zp(-m)
        index = m + NZ // 2
        if kind == 0:
            z_take(0, m)
            for step in onward(0, m):
                z_send(0, m, step)
            y_one(index, chunk, 0, SPLIT)
        elif kind == 1:
            z_take(1, m)
            for step in onward(1, m):
                z_send(1, m, step)
        elif kind == 2:
            y_two(index, chunk, 0, SPLIT)
        elif kind == 3:
            y_end(index, chunk, 0, SPLIT)
            send_sum(chunk)
        elif kind == 4:
            y_two(17, z, SPLIT, CHIP_FEAT)
        elif kind == 5:
            y_end(17, z, SPLIT, CHIP_FEAT)
            for step in onward(1, 0):
                z_send(1, 0, step)
        elif kind == 6:
            sum_squares()
        elif kind == 7:
            find_slots()
        else:
            take_rows()

    for i in range(1, 2 * NX):
        frm = lax.rem(head + i, 2 * NX)
        remote(squares.at[frm], squares.at[frm], sq_s.at[frm], sq_r.at[frm], seq, frm).wait_recv()
    sums = jnp.sum(jnp.sum(squares[...], axis=0), axis=0, keepdims=True) * 0.125
    scale = lax.rsqrt(sums / D + 1e-05)
    for i in range(1, 2 * NX):
        frm = lax.rem(head + i, 2 * NX)
        fx, fc = lax.div(frm, 2), lax.rem(frm, 2)
        for half in (0, 1):
            remote(
                received.at[fx, fc, half], received.at[fx, fc, half],
                sum_s.at[0], sum_r.at[fx, fc, half], seq, frm,
            ).wait_recv()
    kinds = []
    for kind in (0, 1):
        summed = jnp.zeros((HD, ROWS), jnp.float32)
        for fx in range(NX):
            summed += received[fx, kind].reshape(HD, ROWS).astype(jnp.float32)
        scaled = summed * scale
        fresh[kind] = scaled[:, STORED:]
        kinds.append(nt_dot(onehot[...], scaled[:, :STORED].astype(jnp.bfloat16)))
    keys = kinds[0] + empties[...]
    slots = jnp.concatenate(
        [keys.reshape(SESS, CAP, HD), kinds[1].reshape(SESS, CAP, HD)], axis=1
    )
    outgoing[...] = slots.astype(jnp.bfloat16).reshape(NY, NZ, 2 * CAP, HD)

    for i in (2, 1, 3):
        to = yp(i)
        start(remote(outgoing.at[to], by_y.at[NY - i], ry_s.at[i], ry_r.at[NY - i], z * NY + to, head))
    order = [8, 7, 9, 6, 10, 5, 11, 4, 12, 3, 13, 2, 14, 1, 15]
    for i in order:
        to = zp(i)
        start(remote(outgoing.at[y, to], by_z.at[0, z], rz_s.at[0, to], rz_r.at[0, z], to * NY + y, head))
    by_z[0, z] = outgoing[y, z]
    for i in (1, 3, 2):
        remote(by_y.at[i], by_y.at[i], ry_s.at[i], ry_r.at[i], z * NY + yp(i), head).wait_recv()
    for i in order:
        to = zp(i)
        start(remote(
            by_y.at[1:, to], by_z.at[1:, z], rz_s.at[1, to], rz_r.at[1, z], to * NY + y, head
        ))
    by_z[1:, z] = by_y[1:, z]
    fresh_out = pltpu.make_async_copy(fresh, fresh_ref, out_s.at[4])
    fresh_out.start()

    their_weights(kw_ref).wait_send()
    for chunk in range(NZ):
        @pl.when(chunk // 2 != head)
        def _(chunk=chunk):
            remote(
                partial.at[chunk], received.at[x, c, 0],
                sum_s.at[chunk], sum_r.at[x, c, 0], seq, other,
            ).wait_send()
    clock[0] += 1000.0
    drain(0.0)
    outs = []
    for part in (0, 1):
        for i in reversed(order):
            frm = zp(i)
            region = by_z.at[0, frm] if part == 0 else by_z.at[1:, frm]
            remote(region, region, rz_s.at[part, frm], rz_r.at[part, frm], frm * NY + y, head).wait_recv()
        for r in range(NY):
            if (r == 0) == (part == 0):
                outs.append(pltpu.make_async_copy(by_z.at[r], routed_ref.at[:, yp(r)], out_s.at[r]))
                outs[-1].start()
    for copy in outs:
        copy.wait()
    fresh_out.wait()


def project(store_hidden, owner_row, new_hidden, key_columns, value_columns):
    dma = pltpu.SemaphoreType.DMA
    hbm = pl.BlockSpec(memory_space=pltpu.HBM)
    return pl.pallas_call(
        project_kernel,
        out_shape=(
            jax.ShapeDtypeStruct((NZ, NY, 2 * CAP, HD), jnp.bfloat16),
            jax.ShapeDtypeStruct((2, HD, TURN), jnp.float32),
        ),
        in_specs=[hbm] * 5,
        out_specs=(hbm, hbm),
        scratch_shapes=[
            pltpu.VMEM((ROWS, CHIP_FEAT), jnp.bfloat16),
            pltpu.VMEM((1, STORED), jnp.int32),
            pltpu.VMEM((NZ, NY, 16, CHIP_FEAT), jnp.bfloat16),
            pltpu.VMEM((NZ, NY, 16, ROWS), jnp.bfloat16),
            pltpu.VMEM((NX, 2, 2, NY, 16, ROWS), jnp.bfloat16),
            pltpu.VMEM((2 * NX, 8, ROWS), jnp.float32),
            pltpu.VMEM((HIST, STORED), jnp.bfloat16),
            pltpu.VMEM((HIST, HD), jnp.float32),
            pltpu.VMEM((2, HD, TURN), jnp.float32),
            pltpu.VMEM((NY, NZ, 2 * CAP, HD), jnp.bfloat16),
            pltpu.VMEM((NY, NZ, 2 * CAP, HD), jnp.bfloat16),
            pltpu.VMEM((NY, NZ, 2 * CAP, HD), jnp.bfloat16),
            dma((4,)), dma((5,)),
            dma((3,)), dma((3,)),
            dma((2, 17)), dma((2, 17)),
            dma((18, 2, 2)), dma((18, 2, 2)),
            dma((NZ,)), dma((NX, 2, 2)),
            dma((2 * NX,)), dma((2 * NX,)),
            dma((NY,)), dma((NY,)),
            dma((2, NZ)), dma((2, NZ)),
        ],
        compiler_params=pltpu.CompilerParams(
            collective_id=0, has_side_effects=True, vmem_limit_bytes=64 * 1024 * 1024
        ),
        name="project_rows",
    )(store_hidden, owner_row, new_hidden, key_columns, value_columns)


def attend_kernel(
    turn_ref, rows_ref, fresh_ref, query_ref, cos_ref, sin_ref, out_ref, key_ref, value_ref,
    rows_in, fresh_in, query_in, cos_in, sin_in, out, keys_out, values_out, in_s, out_s,
):
    def rotate(values, cosine, sine):
        return values * cosine + pltpu.roll(values, HD // 2, 1) * sine

    fetches = [
        pltpu.make_async_copy(src, dst, in_s.at[i])
        for i, (src, dst) in enumerate((
            (rows_ref, rows_in), (cos_ref, cos_in), (sin_ref, sin_in),
            (fresh_ref, fresh_in), (query_ref, query_in),
        ))
    ]
    for fetch in fetches:
        fetch.start()
    row_at = lax.broadcasted_iota(jnp.int32, (HIST, HIST), 0)
    lane_at = lax.broadcasted_iota(jnp.int32, (HIST, HIST), 1)
    before = jnp.where(lane_at < row_at, 1.0, 0.0).astype(jnp.bfloat16)
    fetches[0].wait()
    rows = rows_in[...].reshape(SESS, 2 * CAP, HD).astype(jnp.float32)
    sent_keys = rows[:, :CAP].reshape(HIST, HD)
    sent_values = rows[:, CAP:].reshape(HIST, HD)
    valid = jnp.abs(sent_keys) < EMPTY_TEST
    sent_keys = jnp.where(valid, sent_keys, 0.0).astype(jnp.bfloat16)
    marks = jnp.where(valid, 1.0, 0.0)
    position = jnp.dot(before, marks.astype(jnp.bfloat16), preferred_element_type=jnp.float32)
    position = jnp.where(valid, position, -1.0).T[:1].astype(jnp.int32)
    place = jnp.where(row_at == position, 1.0, 0.0).astype(jnp.bfloat16)
    history = jnp.dot(
        place,
        jnp.concatenate([sent_keys, sent_values.astype(jnp.bfloat16)], axis=1),
        preferred_element_type=jnp.float32,
    )
    length = jnp.sum(marks[:, :1]).astype(jnp.int32)
    turn = turn_ref[0]
    for fetch in fetches[1:]:
        fetch.wait()

    keys_out[0, :HIST] = rotate(history[:, :HD], cos_in[:HIST], sin_in[:HIST]).astype(jnp.bfloat16)
    values_out[0, :HIST] = history[:, HD:].astype(jnp.bfloat16)
    cosine = cos_in[pl.ds(length, TURN), :]
    sine = sin_in[pl.ds(length, TURN), :]
    live = lax.broadcasted_iota(jnp.int32, (TURN, HD), 0) < turn
    keys_out[0, HIST:] = jnp.where(live, rotate(fresh_in[0].T, cosine, sine), 0.0).astype(jnp.bfloat16)
    values_out[0, HIST:] = jnp.where(live, fresh_in[1].T, 0.0).astype(jnp.bfloat16)
    stores = [
        pltpu.make_async_copy(keys_out, key_ref, out_s.at[0]),
        pltpu.make_async_copy(values_out, value_ref, out_s.at[1]),
    ]
    for copy in stores:
        copy.start()

    keys = keys_out[0]
    values = values_out[0]
    slot_at = lax.broadcasted_iota(jnp.int32, (TURN, CACHE), 0)
    cache_at = lax.broadcasted_iota(jnp.int32, (TURN, CACHE), 1)
    allowed = (cache_at < length) | ((cache_at >= HIST) & (cache_at - HIST <= slot_at))
    for group in range(QH // KVH):
        at = pl.ds(group * HD, HD)
        query = rotate(query_in[:, at].astype(jnp.float32), cosine, sine).astype(jnp.bfloat16)
        scores = nt_dot(query, keys) * (1.0 / math.sqrt(HD))
        scores = jnp.where(allowed, scores, -jnp.inf)
        exponent = jnp.exp(scores - jnp.max(scores, axis=1, keepdims=True))
        weights = (exponent / jnp.sum(exponent, axis=1, keepdims=True)).astype(jnp.bfloat16)
        result = jnp.dot(weights, values, preferred_element_type=jnp.float32)
        out[group] = jnp.where(live, result, 0.0).astype(jnp.bfloat16)
        stores.append(pltpu.make_async_copy(out.at[group], out_ref.at[:, at], out_s.at[2 + group]))
        stores[-1].start()
    for copy in stores:
        copy.wait()


def attend(turn_length, rows, fresh, queries):
    cosine, sine = rotation_tables()
    hbm = pl.BlockSpec(memory_space=pltpu.HBM)
    groups = QH // KVH
    return pl.pallas_call(
        attend_kernel,
        out_shape=(
            jax.ShapeDtypeStruct((TURN, groups * HD), jnp.bfloat16),
            jax.ShapeDtypeStruct((1, CACHE, HD), jnp.bfloat16),
            jax.ShapeDtypeStruct((1, CACHE, HD), jnp.bfloat16),
        ),
        in_specs=[pl.BlockSpec(memory_space=pltpu.SMEM)] + [hbm] * 5,
        out_specs=(hbm, hbm, hbm),
        scratch_shapes=[
            pltpu.VMEM((NZ, NY, 2 * CAP, HD), jnp.bfloat16),
            pltpu.VMEM((2, HD, TURN), jnp.float32),
            pltpu.VMEM((TURN, groups * HD), jnp.bfloat16),
            pltpu.VMEM((CACHE, HD), jnp.float32),
            pltpu.VMEM((CACHE, HD), jnp.float32),
            pltpu.VMEM((groups, TURN, HD), jnp.bfloat16),
            pltpu.VMEM((1, CACHE, HD), jnp.bfloat16),
            pltpu.VMEM((1, CACHE, HD), jnp.bfloat16),
            pltpu.SemaphoreType.DMA((5,)),
            pltpu.SemaphoreType.DMA((2 + groups,)),
        ],
        compiler_params=pltpu.CompilerParams(vmem_limit_bytes=64 * 1024 * 1024),
        name="attend_turn",
    )(turn_length, rows, fresh, queries, jnp.asarray(cosine), jnp.asarray(sine))


def local(store_hidden, owner_map, new_hidden, new_lengths, queries, key_weight, value_weight):
    rows, fresh = project(
        store_hidden, owner_map.reshape(1, STORED), new_hidden, key_weight.T, value_weight.T
    )
    return attend(new_lengths, rows, fresh, queries)


def solution(mesh):
    placed = (
        P("seq", "head"),
        P("seq", None),
        P("seq", "head"),
        P("seq"),
        P("seq", "head"),
        P("head", "seq"),
        P("head", "seq"),
    )
    return jax.shard_map(
        local,
        mesh=mesh,
        in_specs=placed,
        out_specs=(P("seq", "head"), P("seq", None, "head"), P("seq", None, "head")),
        check_vma=False,
    )
```

time: 88.6 us -> 81.4 us (0.919)
  local copies, waits for them, and re-layouts: 5.13 us -> 0 us
  Pallas kernels: 81.8 us -> 80 us
    unnamed x16 -> x0, local copies, waits for them, and re-layouts: 5.13 us -> none
    pallas_call x2, Pallas kernels: 81.8 us -> 80 us  [the longest x1 74 us: project(): pl.pallas_call(project_kernel, out_shape=(jax.ShapeDtypeStruct((NZ, NY, 2...]
where the time goes in v3:
time: 81.4 us; the launch traced here: 81.3 us
  Pallas kernels  80 us (98%)
  between operations  1.29 us (2%)
    pallas_call x1, Pallas kernels, project(): pl.pallas_call(project_kernel, out_shape=(jax.ShapeDtypeStruct((NZ, NY, 2...  74 us
    pallas_call x1, Pallas kernels, attend(): pl.pallas_call(attend_kernel, out_shape=(jax.ShapeDtypeStruct((TURN, grou...  6.02 us

profile of v3, /device:TPU:1, one launch (start us, length us, event | category | flops | bytes accessed | tf_op | source)
XLA Modules:
  0.0 81.3 jit_solution(812458217910568067)
XLA Ops:
  1.3 74.0 %project_rows.1 = (bf16[16,4,16,128]{3,2,1,0:T(8,128)(2,1)}, f32[2,128,128]{2,1,0:T(8,128)}) custom-call(bf16[256,1024]{1,0:T(8,128)(2,1)} %store_ref.1, s32[1,256]{1,0:T(1,128)} %bitcast.5, bf16[128,1024]{1,0:T(8,128)(2,1)} %new_ref.1, bf16[16,1024]{1,0:T(8,128)(2,1)} %bitcast.3, bf16[16,1024]{1,0:T(8,128)(2,1)} %bitcast.4), custom_call_target="tpu_custom_call" | custom-call | tf_op jit(solution)/shard_map/project_rows/pallas_call | solution.py:384
  75.3 6.0 %attend_turn.1 = (bf16[128,1024]{1,0:T(8,128)(2,1)}, bf16[1,640,128]{2,1,0:T(8,128)(2,1)}, bf16[1,640,128]{2,1,0:T(8,128)(2,1)}) custom-call(s32[1]{0:T(128)S(6)} %copy.12.turn_ref, bf16[16,4,16,128]{3,2,1,0:T(8,128)(2,1)} %get-tuple-element.5.rows_ref, f32[2,128,128]{2,1,0:T(8,128)} %get-tuple-element.6.fresh_ref, bf16[128,1024]{1,0:T(8,128)(2,1)} %query_ref.1, ...), custom_call_target="tpu_custom_call" | custom-call | tf_op jit(solution)/shard_map/attend_turn/pallas_call | solution.py:498

commit v4 on v3

--- a/solution.py
+++ b/solution.py
@@ -25,9 +25,9 @@
 CACHE = HIST + TURN
 FEAT = D // (2 * NX)
 CHIP_FEAT = 2 * FEAT
-SPLIT = 1664
-LAG1 = 2.7
-LAG2 = 5.4
+SPLIT = 1536
+WAYS = ((0, 1024), (1024, 2048), (1536, 2048))
+OWN_WAYS = 2
 EMPTY = float(2.0**100)
 EMPTY_TEST = float(2.0**50)
 MESH = pl.DeviceIdType.MESH
@@ -58,7 +58,7 @@
 def project_kernel(
     store_ref, owner_ref, new_ref, kw_ref, vw_ref,
     routed_ref, fresh_ref,
-    xs, owners, gathered, partial, received, squares, onehot, empties, fresh, outgoing, by_y, by_z,
+    xs, owners, gathered, partial, received, squares, onehot, empties, fresh, outgoing, by_y,
     in_s, out_s, core_s, core_r, z_s, z_r, y_s, y_r, sum_s, sum_r, sq_s, sq_r, ry_s, ry_r, rz_s, rz_r,
 ):
     seq = lax.axis_index("seq")
@@ -99,7 +99,7 @@
 
     own = pl.ds(pl.multiple_of(c * FEAT, FEAT), FEAT)
     theirs = pl.ds(pl.multiple_of((1 - c) * FEAT, FEAT), FEAT)
-    mine = gathered.at[z, 0, :, own]
+    mine = gathered.at[0, 0, :, own]
 
     def own_weights(ref):
         return pltpu.make_async_copy(ref, mine, in_s.at[0])
@@ -132,30 +132,53 @@
 
     own_weights(kw_ref).wait()
     remote(
-        kw_ref, gathered.at[z, 0, :, theirs], core_s.at[0], core_r.at[0], seq, other
+        kw_ref, gathered.at[0, 0, :, theirs], core_s.at[0], core_r.at[0], seq, other
     ).wait_recv()
 
-    def z_region(way, chunk):
-        if way == 0:
-            return gathered.at[chunk, 0]
-        return gathered.at[chunk, 1:, :, SPLIT:]
+    far = NZ // 2
+
+    def slot_of(m):
+        if abs(m) == far:
+            return NZ - 1
+        return 2 * m - 1 if m > 0 else -2 * m
+
+    def z_region(way, m):
+        lo, hi = WAYS[way]
+        if way < OWN_WAYS:
+            return gathered.at[slot_of(m), 0, :, lo:hi]
+        return gathered.at[slot_of(m), 1:, :, lo:hi]
 
     def z_send(way, m, step):
-        region = z_region(way, zp(-m))
-        at = m + step + NZ // 2
-        start(remote(region, region, z_s.at[way, at], z_r.at[way, at], zp(step) * NY + y, head))
+        at = m + step + far
+        start(remote(
+            z_region(way, m), z_region(way, m + step),
+            z_s.at[way, at], z_r.at[way, at], zp(step) * NY + y, head,
+        ))
 
     def z_take(way, m):
-        region = z_region(way, zp(-m))
-        at = m + NZ // 2
-        remote(region, region, z_s.at[way, at], z_r.at[way, at], seq, head).wait_recv()
+        region = z_region(way, m)
+        remote(region, region, z_s.at[way, m + far], z_r.at[way, m + far], seq, head).wait_recv()
 
     def onward(way, m):
         if m == 0:
             return [1, -1]
         sign = 1 if m > 0 else -1
-        last = NZ // 2 if sign == (1 if way == 0 else -1) else NZ // 2 - 1
+        last = far if (sign == 1) == (way % 2 == 0) else far - 1
         return [sign] if abs(m) < last else []
+
+    def z_first(way):
+        for step in onward(way, 0):
+            z_send(way, 0, step)
+
+    def z_pass(way, t):
+        for m in (t, -t):
+            if onward(way, m - (1 if m > 0 else -1)):
+                z_take(way, m)
+                for step in onward(way, m):
+                    z_send(way, m, step)
+
+    def chunks_of(t):
+        return slice(slot_of(t), slot_of(t) + (1 if t in (0, far) else 2))
 
     def half_way(lo, hi):
         return lo + (hi - lo) // 256 * 128
@@ -166,26 +189,29 @@
             z * NY + yp(1 if d == 0 else -1), head,
         )
 
-    def y_one(index, chunk, lo, hi):
+    def y_one(index, t, lo, hi):
+        at = chunks_of(t)
         for d in (0, 1):
             start(y_piece(
-                index, 0, d, gathered.at[chunk, 0, :, lo:hi], gathered.at[chunk, 3 - 2 * d, :, lo:hi]
+                index, 0, d, gathered.at[at, 0, :, lo:hi], gathered.at[at, 3 - 2 * d, :, lo:hi]
             ))
 
-    def y_two(index, chunk, lo, hi):
+    def y_two(index, t, lo, hi):
+        at = chunks_of(t)
         mid = half_way(lo, hi)
         for d in (0, 1):
-            whole = gathered.at[chunk, 3 - 2 * d, :, lo:hi]
+            whole = gathered.at[at, 3 - 2 * d, :, lo:hi]
             y_piece(index, 0, d, whole, whole).wait_recv()
             part = slice(lo, mid) if d == 0 else slice(mid, hi)
             start(y_piece(
-                index, 1, d, gathered.at[chunk, 3 - 2 * d, :, part], gathered.at[chunk, 2, :, part]
+                index, 1, d, gathered.at[at, 3 - 2 * d, :, part], gathered.at[at, 2, :, part]
             ))
 
-    def y_end(index, chunk, lo, hi):
+    def y_end(index, t, lo, hi):
+        at = chunks_of(t)
         mid = half_way(lo, hi)
         for d in (0, 1):
-            region = gathered.at[chunk, 2, :, lo:mid] if d == 0 else gathered.at[chunk, 2, :, mid:hi]
+            region = gathered.at[at, 2, :, lo:mid] if d == 0 else gathered.at[at, 2, :, mid:hi]
             y_piece(index, 1, d, region, region).wait_recv()
 
     def sum_squares():
@@ -231,81 +257,64 @@
             region = xs.at[rows, theirs]
             remote(region, region, core_s.at[i], core_r.at[i], seq, other).wait_recv()
 
-    def send_sum(chunk):
+    def sum_send(m):
+        slot = slot_of(m)
+        chunk = zp(-m)
         to = lax.div(chunk, 2)
         half = lax.rem(chunk, 2)
-        result = nt_dot(gathered[chunk].reshape(4 * 16, CHIP_FEAT), xs[...]).astype(jnp.bfloat16)
-        for r in range(NY):
-            partial[chunk, yp(r)] = result[r * 16 : (r + 1) * 16]
-
-        @pl.when(to == head)
-        def _():
-            received[x, c, half] = partial[chunk]
-
-        @pl.when(to != head)
-        def _():
-            remote(
-                partial.at[chunk], received.at[x, c, half],
-                sum_s.at[chunk], sum_r.at[x, c, half], seq, to,
-            ).start()
-
-    arrives = {0: 0.0}
-    todo = [0]
-    while todo:
-        m = todo.pop(0)
-        for step in onward(0, m):
-            arrives[m + step] = arrives[m] + 2.6
-            todo.append(m + step)
-    events = []
-    for m, at in sorted(arrives.items(), key=lambda item: (item[1], item[0])):
-        twin = m if abs(m) != NZ // 2 else -m
-        if m != 0:
-            events.append((at, 0, m))
-            events.append((at + 5.3, 1, twin))
-        events.append((at + LAG1, 2, m))
-        events.append((at + LAG2, 3, m))
-    events.append((2.4, 4, 0))
-    events.append((5.0, 5, 0))
-    events.append((3.0, 6, 0))
-    events.append((5.1, 7, 0))
-    events.append((5.2, 8, 0))
-
-    for step in onward(0, 0):
-        z_send(0, 0, step)
-    y_one(17, z, SPLIT, CHIP_FEAT)
+        return slot, half, to, remote(
+            partial.at[slot], received.at[x, c, half],
+            sum_s.at[slot], sum_r.at[x, c, half], seq, to,
+        )
+
+    def send_sums(t):
+        at = chunks_of(t)
+        count = at.stop - at.start
+        result = nt_dot(gathered[at].reshape(count * 64, CHIP_FEAT), xs[...]).astype(jnp.bfloat16)
+        for i in range(count):
+            m = t if i == 0 else -t
+            slot, half, to, copy = sum_send(m)
+            for r in range(NY):
+                row = i * 64 + r * 16
+                partial[slot, yp(r)] = result[row : row + 16]
+
+            @pl.when(to == head)
+            def _(slot=slot, half=half):
+                received[x, c, half] = partial[slot]
+
+            @pl.when(to != head)
+            def _(copy=copy):
+                copy.start()
+
+    z_first(0)
+    y_one(9, 0, SPLIT, CHIP_FEAT)
+    sum_squares()
+    z_first(1)
+    y_one(0, 0, 0, SPLIT)
     send_rows()
-    y_one(8, z, 0, SPLIT)
-    for at, kind, m in sorted(events):
-        clock[0] = at
+    for s in range(1, far + 3):
+        clock[0] = 2.6 * s
+        if s <= far:
+            z_pass(0, s)
+            if s == 1:
+                y_two(9, 0, SPLIT, CHIP_FEAT)
+            z_pass(1, s)
+            y_one(s, s, 0, SPLIT)
+        if s == 2:
+            y_end(9, 0, SPLIT, CHIP_FEAT)
+            for way in range(OWN_WAYS, len(WAYS)):
+                z_first(way)
+            find_slots()
+            take_rows()
+        elif 1 <= s - 2 <= far:
+            for way in range(OWN_WAYS, len(WAYS)):
+                z_pass(way, s - 2)
+        if s - 1 <= far:
+            y_two(s - 1, s - 1, 0, SPLIT)
+        if s >= 2:
+            y_end(s - 2, s - 2, 0, SPLIT)
+            send_sums(s - 2)
         drain(6.0)
-        chunk = zp(-m)
-        index = m + NZ // 2
-        if kind == 0:
-            z_take(0, m)
-            for step in onward(0, m):
-                z_send(0, m, step)
-            y_one(index, chunk, 0, SPLIT)
-        elif kind == 1:
-            z_take(1, m)
-            for step in onward(1, m):
-                z_send(1, m, step)
-        elif kind == 2:
-            y_two(index, chunk, 0, SPLIT)
-        elif kind == 3:
-            y_end(index, chunk, 0, SPLIT)
-            send_sum(chunk)
-        elif kind == 4:
-            y_two(17, z, SPLIT, CHIP_FEAT)
-        elif kind == 5:
-            y_end(17, z, SPLIT, CHIP_FEAT)
-            for step in onward(1, 0):
-                z_send(1, 0, step)
-        elif kind == 6:
-            sum_squares()
-        elif kind == 7:
-            find_slots()
-        else:
-            take_rows()
 
     for i in range(1, 2 * NX):
         frm = lax.rem(head + i, 2 * NX)
@@ -340,39 +349,36 @@
     order = [8, 7, 9, 6, 10, 5, 11, 4, 12, 3, 13, 2, 14, 1, 15]
     for i in order:
         to = zp(i)
-        start(remote(outgoing.at[y, to], by_z.at[0, z], rz_s.at[0, to], rz_r.at[0, z], to * NY + y, head))
-    by_z[0, z] = outgoing[y, z]
+        start(remote(
+            outgoing.at[y, to], routed_ref.at[0, z], rz_s.at[0, to], rz_r.at[0, z], to * NY + y, head
+        ))
     for i in (1, 3, 2):
         remote(by_y.at[i], by_y.at[i], ry_s.at[i], ry_r.at[i], z * NY + yp(i), head).wait_recv()
     for i in order:
         to = zp(i)
         start(remote(
-            by_y.at[1:, to], by_z.at[1:, z], rz_s.at[1, to], rz_r.at[1, z], to * NY + y, head
+            by_y.at[1:, to], routed_ref.at[1:, z], rz_s.at[1, to], rz_r.at[1, z], to * NY + y, head
         ))
-    by_z[1:, z] = by_y[1:, z]
+    outs = [
+        pltpu.make_async_copy(outgoing.at[y, z], routed_ref.at[0, z], out_s.at[0]),
+        pltpu.make_async_copy(by_y.at[1:, z], routed_ref.at[1:, z], out_s.at[1]),
+    ]
+    for copy in outs:
+        copy.start()
     fresh_out = pltpu.make_async_copy(fresh, fresh_ref, out_s.at[4])
     fresh_out.start()
 
     their_weights(kw_ref).wait_send()
-    for chunk in range(NZ):
-        @pl.when(chunk // 2 != head)
-        def _(chunk=chunk):
-            remote(
-                partial.at[chunk], received.at[x, c, 0],
-                sum_s.at[chunk], sum_r.at[x, c, 0], seq, other,
-            ).wait_send()
+    for m in range(1 - far, far + 1):
+        _, _, to, copy = sum_send(m)
+        pl.when(to != head)(copy.wait_send)
     clock[0] += 1000.0
     drain(0.0)
-    outs = []
     for part in (0, 1):
         for i in reversed(order):
             frm = zp(i)
-            region = by_z.at[0, frm] if part == 0 else by_z.at[1:, frm]
+            region = routed_ref.at[0, frm] if part == 0 else routed_ref.at[1:, frm]
             remote(region, region, rz_s.at[part, frm], rz_r.at[part, frm], frm * NY + y, head).wait_recv()
-        for r in range(NY):
-            if (r == 0) == (part == 0):
-                outs.append(pltpu.make_async_copy(by_z.at[r], routed_ref.at[:, yp(r)], out_s.at[r]))
-                outs[-1].start()
     for copy in outs:
         copy.wait()
     fresh_out.wait()
@@ -384,7 +390,7 @@
     return pl.pallas_call(
         project_kernel,
         out_shape=(
-            jax.ShapeDtypeStruct((NZ, NY, 2 * CAP, HD), jnp.bfloat16),
+            jax.ShapeDtypeStruct((NY, NZ, 2 * CAP, HD), jnp.bfloat16),
             jax.ShapeDtypeStruct((2, HD, TURN), jnp.float32),
         ),
         in_specs=[hbm] * 5,
@@ -401,11 +407,10 @@
             pltpu.VMEM((2, HD, TURN), jnp.float32),
             pltpu.VMEM((NY, NZ, 2 * CAP, HD), jnp.bfloat16),
             pltpu.VMEM((NY, NZ, 2 * CAP, HD), jnp.bfloat16),
-            pltpu.VMEM((NY, NZ, 2 * CAP, HD), jnp.bfloat16),
             dma((4,)), dma((5,)),
             dma((3,)), dma((3,)),
-            dma((2, 17)), dma((2, 17)),
-            dma((18, 2, 2)), dma((18, 2, 2)),
+            dma((len(WAYS), NZ + 1)), dma((len(WAYS), NZ + 1)),
+            dma((10, 2, 2)), dma((10, 2, 2)),
             dma((NZ,)), dma((NX, 2, 2)),
             dma((2 * NX,)), dma((2 * NX,)),
             dma((NY,)), dma((NY,)),
@@ -425,19 +430,21 @@
     def rotate(values, cosine, sine):
         return values * cosine + pltpu.roll(values, HD // 2, 1) * sine
 
+    y = lax.rem(lax.axis_index("seq"), NY)
     fetches = [
         pltpu.make_async_copy(src, dst, in_s.at[i])
-        for i, (src, dst) in enumerate((
-            (rows_ref, rows_in), (cos_ref, cos_in), (sin_ref, sin_in),
-            (fresh_ref, fresh_in), (query_ref, query_in),
-        ))
+        for i, (src, dst) in enumerate(
+            [(rows_ref.at[r], rows_in.at[:, lax.rem(y + r, NY)]) for r in range(NY)]
+            + [(cos_ref, cos_in), (sin_ref, sin_in), (fresh_ref, fresh_in), (query_ref, query_in)]
+        )
     ]
     for fetch in fetches:
         fetch.start()
     row_at = lax.broadcasted_iota(jnp.int32, (HIST, HIST), 0)
     lane_at = lax.broadcasted_iota(jnp.int32, (HIST, HIST), 1)
     before = jnp.where(lane_at < row_at, 1.0, 0.0).astype(jnp.bfloat16)
-    fetches[0].wait()
+    for fetch in fetches[:NY]:
+        fetch.wait()
     rows = rows_in[...].reshape(SESS, 2 * CAP, HD).astype(jnp.float32)
     sent_keys = rows[:, :CAP].reshape(HIST, HD)
     sent_values = rows[:, CAP:].reshape(HIST, HD)
@@ -454,7 +461,7 @@
     )
     length = jnp.sum(marks[:, :1]).astype(jnp.int32)
     turn = turn_ref[0]
-    for fetch in fetches[1:]:
+    for fetch in fetches[NY:]:
         fetch.wait()
 
     keys_out[0, :HIST] = rotate(history[:, :HD], cos_in[:HIST], sin_in[:HIST]).astype(jnp.bfloat16)
@@ -479,11 +486,12 @@
     for group in range(QH // KVH):
         at = pl.ds(group * HD, HD)
         query = rotate(query_in[:, at].astype(jnp.float32), cosine, sine).astype(jnp.bfloat16)
-        scores = nt_dot(query, keys) * (1.0 / math.sqrt(HD))
-        scores = jnp.where(allowed, scores, -jnp.inf)
-        exponent = jnp.exp(scores - jnp.max(scores, axis=1, keepdims=True))
-        weights = (exponent / jnp.sum(exponent, axis=1, keepdims=True)).astype(jnp.bfloat16)
-        result = jnp.dot(weights, values, preferred_element_type=jnp.float32)
+        scores = jnp.where(allowed, nt_dot(query, keys), -jnp.inf)
+        highest = jnp.max(scores, axis=1, keepdims=True)
+        exponent = jnp.exp2((scores - highest) * (math.log2(math.e) / math.sqrt(HD)))
+        total = jnp.sum(exponent, axis=1, keepdims=True)
+        result = jnp.dot(exponent.astype(jnp.bfloat16), values, preferred_element_type=jnp.float32)
+        result = result * (1.0 / total)
         out[group] = jnp.where(live, result, 0.0).astype(jnp.bfloat16)
         stores.append(pltpu.make_async_copy(out.at[group], out_ref.at[:, at], out_s.at[2 + group]))
         stores[-1].start()
@@ -513,7 +521,7 @@
             pltpu.VMEM((groups, TURN, HD), jnp.bfloat16),
             pltpu.VMEM((1, CACHE, HD), jnp.bfloat16),
             pltpu.VMEM((1, CACHE, HD), jnp.bfloat16),
-            pltpu.SemaphoreType.DMA((5,)),
+            pltpu.SemaphoreType.DMA((4 + NY,)),
             pltpu.SemaphoreType.DMA((2 + groups,)),
         ],
         compiler_params=pltpu.CompilerParams(vmem_limit_bytes=64 * 1024 * 1024),

time: 81.4 us -> 79.3 us (0.974)
  Pallas kernels: 80 us -> 77.9 us
    pallas_call x1, Pallas kernels: 74 us -> 72.5 us  [project(): pl.pallas_call(project_kernel, out_shape=(jax.ShapeDtypeStruct((NY, NZ, 2...]
where the time goes in v4:
time: 79.3 us; the launch traced here: 79.2 us
  Pallas kernels  77.9 us (98%)
  between operations  1.29 us (2%)
    pallas_call x1, Pallas kernels, project(): pl.pallas_call(project_kernel, out_shape=(jax.ShapeDtypeStruct((NY, NZ, 2...  72.5 us
    pallas_call x1, Pallas kernels, attend(): pl.pallas_call(attend_kernel, out_shape=(jax.ShapeDtypeStruct((TURN, grou...  5.38 us

profile of v4, /device:TPU:1, one launch (start us, length us, event | category | flops | bytes accessed | tf_op | source)
XLA Modules:
  0.0 79.2 jit_solution(16023259784274122778)
XLA Ops:
  1.3 72.5 %project_rows.1 = (bf16[4,16,16,128]{3,2,1,0:T(8,128)(2,1)}, f32[2,128,128]{2,1,0:T(8,128)}) custom-call(bf16[256,1024]{1,0:T(8,128)(2,1)} %store_ref.1, s32[1,256]{1,0:T(1,128)} %bitcast.5, bf16[128,1024]{1,0:T(8,128)(2,1)} %new_ref.1, bf16[16,1024]{1,0:T(8,128)(2,1)} %bitcast.3, bf16[16,1024]{1,0:T(8,128)(2,1)} %bitcast.4), custom_call_target="tpu_custom_call" | custom-call | tf_op jit(solution)/shard_map/project_rows/pallas_call | solution.py:390
  73.8 5.4 %attend_turn.1 = (bf16[128,1024]{1,0:T(8,128)(2,1)}, bf16[1,640,128]{2,1,0:T(8,128)(2,1)}, bf16[1,640,128]{2,1,0:T(8,128)(2,1)}) custom-call(s32[1]{0:T(128)S(6)} %copy.12.turn_ref, bf16[4,16,16,128]{3,2,1,0:T(8,128)(2,1)} %get-tuple-element.5.rows_ref, f32[2,128,128]{2,1,0:T(8,128)} %get-tuple-element.6.fresh_ref, bf16[128,1024]{1,0:T(8,128)(2,1)} %query_ref.1, ...), custom_call_target="tpu_custom_call" | custom-call | tf_op jit(solution)/shard_map/attend_turn/pallas_call | solution.py:506

commit v5 on v4

--- a/solution.py
+++ b/solution.py
@@ -354,11 +354,16 @@
         ))
     for i in (1, 3, 2):
         remote(by_y.at[i], by_y.at[i], ry_s.at[i], ry_r.at[i], z * NY + yp(i), head).wait_recv()
-    for i in order:
-        to = zp(i)
-        start(remote(
-            by_y.at[1:, to], routed_ref.at[1:, z], rz_s.at[1, to], rz_r.at[1, z], to * NY + y, head
-        ))
+    for group in (order[:3], order[3:7], order[7:]):
+        copies = []
+        for i in group:
+            to = zp(i)
+            copies.append(remote(
+                by_y.at[1:, to], routed_ref.at[1:, z], rz_s.at[1, to], rz_r.at[1, z], to * NY + y, head
+            ))
+            copies[-1].start()
+        for copy in copies:
+            copy.wait_send()
     outs = [
         pltpu.make_async_copy(outgoing.at[y, z], routed_ref.at[0, z], out_s.at[0]),
         pltpu.make_async_copy(by_y.at[1:, z], routed_ref.at[1:, z], out_s.at[1]),

time: 79.3 us -> 78.8 us (level)
  no operation moved by 1% of the time
where the time goes in v5:
time: 78.8 us; the launch traced here: 78.7 us
  Pallas kernels  77.4 us (98%)
  between operations  1.29 us (2%)
    pallas_call x1, Pallas kernels, project(): pl.pallas_call(project_kernel, out_shape=(jax.ShapeDtypeStruct((NY, NZ, 2...  72 us
    pallas_call x1, Pallas kernels, attend(): pl.pallas_call(attend_kernel, out_shape=(jax.ShapeDtypeStruct((TURN, grou...  5.38 us

profile of v5, /device:TPU:1, one launch (start us, length us, event | category | flops | bytes accessed | tf_op | source)
XLA Modules:
  0.0 78.7 jit_solution(8105716698815441741)
XLA Ops:
  1.3 72.0 %project_rows.1 = (bf16[4,16,16,128]{3,2,1,0:T(8,128)(2,1)}, f32[2,128,128]{2,1,0:T(8,128)}) custom-call(bf16[256,1024]{1,0:T(8,128)(2,1)} %store_ref.1, s32[1,256]{1,0:T(1,128)} %bitcast.5, bf16[128,1024]{1,0:T(8,128)(2,1)} %new_ref.1, bf16[16,1024]{1,0:T(8,128)(2,1)} %bitcast.3, bf16[16,1024]{1,0:T(8,128)(2,1)} %bitcast.4), custom_call_target="tpu_custom_call" | custom-call | tf_op jit(solution)/shard_map/project_rows/pallas_call | solution.py:395
  73.3 5.4 %attend_turn.1 = (bf16[128,1024]{1,0:T(8,128)(2,1)}, bf16[1,640,128]{2,1,0:T(8,128)(2,1)}, bf16[1,640,128]{2,1,0:T(8,128)(2,1)}) custom-call(s32[1]{0:T(128)S(6)} %copy.12.turn_ref, bf16[4,16,16,128]{3,2,1,0:T(8,128)(2,1)} %get-tuple-element.5.rows_ref, f32[2,128,128]{2,1,0:T(8,128)} %get-tuple-element.6.fresh_ref, bf16[128,1024]{1,0:T(8,128)(2,1)} %query_ref.1, ...), custom_call_target="tpu_custom_call" | custom-call | tf_op jit(solution)/shard_map/attend_turn/pallas_call | solution.py:511
